TPU v7x, 256 devices: a whole 4x4x8 slice. The times are simulated.
256 devices in a mesh: dp: 16 (over z, core), section: 4 (over x), mp: 4 (over y).
Axes of the slice: x: 4, y: 4, z: 8, core: 2. Of those that a mesh axis runs over, the one named last changes fastest.
Arguments:
- patches: bfloat16 [2, 1536, 1280], P(None, 'dp'), may hold values from -6 to 6
- image_sizes: int32 [2, 16, 4], P(None, 'dp'), may hold values from 1 to 18, as said below
- raster_order: int32 [2, 384], P(None, 'dp'), may hold values from 0 to 23, as said below
- image_starts: int32 [2, 16, 4], P(None, 'dp'), may hold values from 1 to 255, as said below
- qkv_weight: bfloat16 [4, 1280, 3840], P('section', 'dp', 'mp'), may hold values from -0.15625 to 0.15625
- proj_weight: bfloat16 [4, 1280, 1280], P('section', 'mp', 'dp'), may hold values from -0.15625 to 0.15625
- merge_in: bfloat16 [5120, 5120], P(None, ('section', 'mp')), may hold values from -0.078125 to 0.078125
- merge_out: bfloat16 [5120, 8192], P(('section', 'mp')), may hold values from -0.125 to 0.125
- text_embeds: bfloat16 [2, 4096, 8192], P(None, 'dp', ('section', 'mp')), may hold values from -6 to 6
- joined_grad: bfloat16 [2, 4096, 8192], P(None, 'dp', ('section', 'mp')), may hold values from -6 to 6
Outputs:
- joined: bfloat16 [2, 4096, 8192], P(None, 'dp', ('section', 'mp'))
- qkv_grad: float32 [4, 1280, 3840], P('section', 'dp', 'mp')
- proj_grad: float32 [4, 1280, 1280], P('section', 'mp', 'dp')
- merge_in_grad: float32 [5120, 5120], P('dp', ('section', 'mp'))
- merge_out_grad: float32 [5120, 8192], P(('section', 'mp'), 'dp')
Inputs may be any that keep to these rules, and one draw needn't show every extreme that they name: `image_sizes`: for each micro-batch and data rank the 4 sizes sum to 24, and one of them is 18. `raster_order`: within each data rank's block of 24, a permutation that maps every image's span of places onto itself. `image_starts`: increasing within a rank's 4 images; the first is 1; each image's positions end at or before the next image's start; the last image's positions end at 256.
All inputs are finite; a program needn't handle non-finite values.
Results may differ from a plain program's by a relative error of at most 0.038.
Values may be sent and summed in bfloat16 or wider, within the bound.
No kernel may reach another device: no remote copies, remote signals or barrier semaphores. Data moves between devices by JAX's collectives and lax.ppermute only.
A program may use at most 128 MiB of HBM per device.

v0:
```python
import functools
import math

import jax
import jax.numpy as jnp
from jax import lax
from jax.experimental import pallas as pl
from jax.experimental.pallas import tpu as pltpu
from jax.sharding import PartitionSpec as P

HEADS_VIS = 16
WINDOW = 16
EPSILON = 1e-06

QUARTERS = 4
SECTIONS = 4
HEADS = HEADS_VIS // QUARTERS
HEAD = 80
WIDTH = 1280
MERGED = 24
TOKENS = 2 * MERGED
ROWS = QUARTERS * TOKENS
QKV = 3 * HEADS * HEAD
MIX = HEADS * HEAD
PROJ_AT = 1024
JOINT = PROJ_AT + MIX
HIDDEN = 320
FEATURES = 512
SCALE = HEAD ** (-0.5)

bf16 = jnp.bfloat16
f32 = jnp.float32


def permute(value, pairs):
    return lax.ppermute(value, ("section", "mp"), pairs)


def across(source, target, steps=0):
    return [
        (QUARTERS * source + m, QUARTERS * target + (m + steps) % QUARTERS)
        for m in range(QUARTERS)
    ]


def to_section(value, source, target):
    return [permute(value, across(source, target, step)) for step in range(QUARTERS)]


def exchange(value):
    return lax.all_to_all(value, "mp", 0, 0)


def everyones(value):
    return exchange(jnp.broadcast_to(value[None], (QUARTERS, *value.shape)))


def dot(a, b):
    return lax.dot_general(a, b, (((1,), (0,)), ((), ())), preferred_element_type=f32)


def dot_nt(a, b):
    return lax.dot_general(a, b, (((1,), (1,)), ((), ())), preferred_element_type=f32)


def dot_tn(a, b):
    return lax.dot_general(a, b, (((0,), (0,)), ((), ())), preferred_element_type=f32)


def unit_rows(values):
    return values * lax.rsqrt(jnp.mean(values * values, axis=-1, keepdims=True) + EPSILON)


def unit_back(values, cotangent):
    inverse = lax.rsqrt(jnp.mean(values * values, axis=-1, keepdims=True) + EPSILON)
    along = jnp.mean(cotangent * values, axis=-1, keepdims=True)
    return inverse * cotangent - values * (inverse * inverse * inverse * along)


def image_layout(image_sizes):
    span_ends = jnp.cumsum(image_sizes, dtype=jnp.int32)
    span_starts = span_ends - image_sizes
    places = jnp.arange(MERGED, dtype=jnp.int32)
    image_of = jnp.sum(
        (places[:, None] >= span_ends[None, :]).astype(jnp.int32), axis=1, dtype=jnp.int32
    )
    onehot = image_of[:, None] == jnp.arange(image_sizes.shape[0], dtype=jnp.int32)[None, :]
    offset = jnp.sum(jnp.where(onehot, span_starts[None, :], 0), axis=1, dtype=jnp.int32)
    return (image_of, places - offset, onehot)


def gather_blocks(place_ref, blocks, held, turned):
    for step in range(QUARTERS):
        if turned:
            owner = lax.rem(place_ref[0] - step + QUARTERS, QUARTERS)
            rows = pl.ds(pl.multiple_of(owner * TOKENS, 16), TOKENS)
        else:
            rows = slice(step * TOKENS, (step + 1) * TOKENS)
        held[rows, :] = blocks[step][...]


def head_parts(projected, head):
    at = 3 * HEAD * head
    return (
        projected[:, at : at + HEAD],
        projected[:, at + HEAD : at + 2 * HEAD],
        projected[:, at + 2 * HEAD : at + 3 * HEAD],
    )


def head_weights(queries, keys, same):
    scores = jnp.where(same, dot_nt(queries, keys) * SCALE, -1000000000.0)
    raised = jnp.exp(scores - jnp.max(scores, axis=-1, keepdims=True))
    return raised / jnp.sum(raised, axis=-1, keepdims=True)


def inner_rows(held, weight, same):
    normed = unit_rows(held[...].astype(f32)).astype(bf16)
    projected = dot(normed, weight[:, :QKV]).astype(bf16)
    mixed = []
    for head in range(HEADS):
        queries, keys, values = head_parts(projected, head)
        mixed.append(dot(head_weights(queries, keys, same).astype(bf16), values).astype(bf16))
    return normed, projected, jnp.concatenate(mixed, axis=1)


def forward_kernel(place_ref, down, across_ref, x0, x1, x2, x3, weight, part, held, *, turned):
    gather_blocks(place_ref, (x0, x1, x2, x3), held, turned)
    same = down[...] == across_ref[...]
    _, _, mixed = inner_rows(held, weight, same)
    total = dot_nt(mixed, weight[:, PROJ_AT:]).astype(bf16)
    for quarter in range(QUARTERS):
        part[quarter] = total[quarter * TOKENS : (quarter + 1) * TOKENS]


def keep_kernel(place_ref, down, across_ref, x0, x1, x2, x3, weight, normed, projected, mixed, held):
    gather_blocks(place_ref, (x0, x1, x2, x3), held, True)
    same = down[...] == across_ref[...]
    normed[...], projected[...], mixed[...] = inner_rows(held, weight, same)


def grad_heads(grad_out, projected, weight, same):
    grad_mixed = dot(grad_out, weight[:, PROJ_AT:]).astype(bf16)
    pieces = []
    for head in range(HEADS):
        queries, keys, values = head_parts(projected, head)
        weights = head_weights(queries, keys, same)
        grad_head = grad_mixed[:, HEAD * head : HEAD * (head + 1)]
        grad_values = dot_tn(weights.astype(bf16), grad_head)
        grad_weights = dot_nt(grad_head, values).astype(bf16).astype(f32)
        centre = jnp.sum(grad_weights * weights, axis=-1, keepdims=True)
        grad_scores = (weights * (grad_weights - centre) * SCALE).astype(bf16)
        pieces += [dot(grad_scores, keys), dot_tn(grad_scores, queries), grad_values]
    return jnp.concatenate([piece.astype(bf16) for piece in pieces], axis=1)


def backward_kernel(
    place_ref,
    down,
    across_ref,
    g0,
    g1,
    g2,
    g3,
    projected,
    weight,
    g_before,
    p_before,
    g_after,
    p_after,
    part,
    held,
    *,
    turned,
):
    gather_blocks(place_ref, (g0, g1, g2, g3), held, turned)
    same = down[...] == across_ref[...]
    grad_out = held[...]
    grad_projected = grad_heads(grad_out, projected[...], weight, same)
    total = dot_nt(grad_projected, weight[:, :QKV]).astype(bf16)
    for quarter in range(QUARTERS):
        part[quarter] = total[quarter * TOKENS : (quarter + 1) * TOKENS]
    g_after[...] = g_before[...] + grad_out
    p_after[...] = p_before[...] + grad_projected


def last_kernel(
    place_ref,
    down,
    across_ref,
    g0,
    g1,
    g2,
    g3,
    projected,
    weight,
    g_before,
    p_before,
    normed,
    mixed,
    joint_grad,
    held,
):
    gather_blocks(place_ref, (g0, g1, g2, g3), held, True)
    same = down[...] == across_ref[...]
    grad_projected = p_before[...] + grad_heads(held[...], projected[...], weight, same)
    step = WIDTH // 5
    for at in range(0, WIDTH, step):
        rows = slice(at, at + step)
        joint_grad[rows, :QKV] = dot_tn(normed[:, rows], grad_projected).astype(bf16)
        joint_grad[rows, QKV:PROJ_AT] = jnp.zeros((step, PROJ_AT - QKV), bf16)
        grad_rows = g_before[:, rows] + held[:, rows]
        joint_grad[rows, PROJ_AT:] = dot_tn(grad_rows, mixed[...]).astype(bf16)


def merge_kernel(_, blocks, weight, grad_act, merged, activated, grad_before, part):
    before = jnp.zeros((TOKENS, HIDDEN), f32)
    for quarter in range(QUARTERS):
        at = slice(quarter * WIDTH, (quarter + 1) * WIDTH)
        normed = unit_rows(blocks[quarter].astype(f32)).astype(bf16)
        merged[:, at] = normed
        before = before + dot(normed, weight[at, :])
    tail = 0.5 * (1.0 + lax.erf(before * math.sqrt(0.5)))
    bell = jnp.exp(-0.5 * before * before) * (1.0 / math.sqrt(2.0 * math.pi))
    activated[...] = (before * tail).astype(bf16)
    grad = ((tail + before * bell) * grad_act[...]).astype(bf16)
    grad_before[...] = grad
    for quarter in range(QUARTERS):
        at = slice(quarter * WIDTH, (quarter + 1) * WIDTH)
        part[quarter] = dot_nt(grad, weight[at, :]).astype(bf16)


def merger_grad_kernel(merged, grad_before, activated, visual_grad, out):
    out[0, :, :FEATURES] = dot_tn(activated[...], visual_grad[0]).astype(bf16)
    out[0, :, FEATURES:] = dot_tn(merged[0], grad_before[...]).astype(bf16)


def merger_grads(merged, grad_before, activated, visual_grad):
    whole = pl.BlockSpec((TOKENS, HIDDEN), lambda j: (0, 0))
    return pl.pallas_call(
        merger_grad_kernel,
        grid=(16,),
        in_specs=[
            pl.BlockSpec((1, TOKENS, HIDDEN), lambda j: (j, 0, 0)),
            whole,
            whole,
            pl.BlockSpec((1, TOKENS, FEATURES), lambda j: (j, 0, 0)),
        ],
        out_specs=pl.BlockSpec((1, HIDDEN, FEATURES + HIDDEN), lambda j: (j, 0, 0)),
        out_shape=jax.ShapeDtypeStruct((16, HIDDEN, FEATURES + HIDDEN), bf16),
        compiler_params=pltpu.CompilerParams(vmem_limit_bytes=16 * 1024 * 1024),
        cost_estimate=pl.CostEstimate(
            flops=2 * TOKENS * 16 * HIDDEN * (FEATURES + HIDDEN),
            bytes_accessed=4 * 16 * HIDDEN * (FEATURES + HIDDEN),
            transcendentals=0,
        ),
    )(merged, grad_before, activated, visual_grad)


def call(kernel, operands, results, scratch, flops, moved):
    return pl.pallas_call(
        kernel,
        in_specs=[pl.BlockSpec(memory_space=pltpu.SMEM)]
        + [pl.BlockSpec(memory_space=pltpu.VMEM)] * (len(operands) - 1),
        out_specs=[pl.BlockSpec(memory_space=pltpu.VMEM)] * len(results),
        out_shape=[jax.ShapeDtypeStruct(shape, kind) for shape, kind in results],
        scratch_shapes=[pltpu.VMEM(shape, kind) for shape, kind in scratch],
        compiler_params=pltpu.CompilerParams(vmem_limit_bytes=40 * 1024 * 1024),
        cost_estimate=pl.CostEstimate(flops=flops, bytes_accessed=moved, transcendentals=0),
    )(*operands)


PART = ((QUARTERS, TOKENS, WIDTH), bf16)


def local(
    patches,
    image_sizes,
    raster_order,
    image_starts,
    qkv_weight,
    proj_weight,
    merge_in,
    merge_out,
    text_embeds,
    joined_grad,
):
    section = lax.axis_index("section")
    place = lax.axis_index("mp")
    place_ref = place.reshape(1)
    is_last = section == SECTIONS - 1

    joint_local = jnp.concatenate(
        [qkv_weight[0], jnp.zeros((WIDTH // 16, PROJ_AT - QKV), bf16), proj_weight[0].T], axis=1
    )
    joint = lax.all_gather(joint_local, "dp", axis=0, tiled=True)

    marks = []
    spots = []
    for micro in range(2):
        image_of, within, onehot = image_layout(image_sizes[micro, 0])
        window_of = image_of * MERGED + within // WINDOW
        marks.append(jnp.where(is_last, image_of, window_of) + micro * 1024)
        starts = jnp.where(onehot, image_starts[micro, 0][None, :], 0)
        slots = jnp.sum(starts, axis=1, dtype=jnp.int32) + within
        order = raster_order[micro]
        from_raster = order[None, :] == jnp.arange(MERGED, dtype=jnp.int32)[:, None]
        spots.append(jnp.sum(jnp.where(from_raster, slots[None, :], 0), axis=1, dtype=jnp.int32))
    mark = jnp.tile(jnp.concatenate(marks), QUARTERS)
    down, right = mark[:, None], mark[None, :]
    positions = jnp.arange(text_embeds.shape[1], dtype=jnp.int32)
    chosen = jnp.stack(spots)[:, :, None] == positions[None, None, :]
    chosen_bf = chosen.astype(bf16)

    visual_grad = jnp.einsum(
        "mts,msf->mtf", chosen_bf, joined_grad, preferred_element_type=f32
    ).astype(bf16)
    visual_grad = visual_grad.reshape(TOKENS, FEATURES)
    visual_grad_full = lax.all_gather(visual_grad, ("section", "mp"), axis=0)
    grad_act = jnp.einsum(
        "jtf,rjf->tr",
        visual_grad_full,
        merge_out.reshape(HIDDEN, 16, FEATURES),
        preferred_element_type=f32,
    )

    quarters = jnp.swapaxes(patches.reshape(TOKENS, QUARTERS, WIDTH), 0, 1)
    quarters, visual_grad_full, grad_act = lax.optimization_barrier(
        (quarters, visual_grad_full, grad_act)
    )
    first = section == 0
    blocks = [quarters[quarter] for quarter in range(QUARTERS)]
    own = lax.dynamic_index_in_dim(quarters, place, 0, False)
    saved = [
        lax.dynamic_index_in_dim(quarters, (place + QUARTERS - step) % QUARTERS, 0, False)
        for step in range(QUARTERS)
    ]
    saved = [jnp.where(first, block, jnp.zeros_like(block)) for block in saved]

    layer_flops = 2 * ROWS * WIDTH * JOINT
    layer_bytes = 2 * WIDTH * JOINT + 8 * ROWS * WIDTH
    held = ((ROWS, WIDTH), bf16)
    for stage in range(SECTIONS):
        (terms,) = call(
            functools.partial(forward_kernel, turned=stage > 0),
            [place_ref, down, right, *blocks, joint],
            [PART],
            [held],
            layer_flops,
            layer_bytes,
        )
        total = own.astype(f32) + jnp.sum(exchange(terms).astype(f32), axis=0)
        own = total.astype(bf16)
        if stage < SECTIONS - 1:
            blocks = to_section(own, stage, stage + 1)
            saved = [old + new for old, new in zip(saved, blocks)]
            own = blocks[0]

    sent = [permute(own, across(SECTIONS - 1, target)) for target in range(SECTIONS - 1)]
    own = jnp.where(is_last, own, sent[0] + sent[1] + sent[2])
    merged, activated, grad_before, terms = call(
        merge_kernel,
        [place_ref, everyones(own), merge_in, grad_act],
        [
            ((TOKENS, QUARTERS * WIDTH), bf16),
            ((TOKENS, HIDDEN), bf16),
            ((TOKENS, HIDDEN), bf16),
            PART,
        ],
        [],
        4 * TOKENS * QUARTERS * WIDTH * HIDDEN,
        2 * QUARTERS * WIDTH * HIDDEN,
    )
    normed, projected, mixed = call(
        keep_kernel,
        [place_ref, down, right, *saved, joint],
        [((ROWS, WIDTH), bf16), ((ROWS, QKV), bf16), ((ROWS, MIX), bf16)],
        [held],
        layer_flops,
        layer_bytes,
    )

    total = jnp.sum(exchange(terms).astype(f32), axis=0)
    leaving = total.astype(bf16)
    leaving, merged, normed = lax.optimization_barrier((leaving, merged, normed))
    arrived = [permute(leaving, across(s, SECTIONS - 1)) for s in range(SECTIONS - 1)]
    merged = jnp.swapaxes(merged.reshape(TOKENS, 16, HIDDEN), 0, 1)
    merger_grad = merger_grads(merged, grad_before, activated, visual_grad_full)
    *arrived, merger_grad = lax.optimization_barrier((*arrived, merger_grad))
    merger_grad = lax.psum_scatter(merger_grad, "dp", scatter_dimension=0, tiled=False)
    for term in arrived:
        total = total + term.astype(f32)
    grad_own = unit_back(own.astype(f32), total)
    grad_own = jnp.where(is_last, grad_own, 0.0).astype(bf16)

    grad_rows = jnp.zeros((ROWS, WIDTH), bf16)
    grad_projected = jnp.zeros((ROWS, QKV), bf16)
    gathered = everyones(grad_own)
    grads = [gathered[quarter] for quarter in range(QUARTERS)]
    for layer in range(SECTIONS - 1, 0, -1):
        grad_rows, grad_projected, terms = call(
            functools.partial(backward_kernel, turned=layer < SECTIONS - 1),
            [place_ref, down, right, *grads, projected, joint, grad_rows, grad_projected],
            [((ROWS, WIDTH), bf16), ((ROWS, QKV), bf16), PART],
            [held],
            layer_flops,
            layer_bytes,
        )
        total = jnp.sum(exchange(terms).astype(f32), axis=0)
        grad_own = grad_own.astype(f32) + unit_back(saved[0].astype(f32), total)
        grads = to_section(grad_own.astype(bf16), layer, layer - 1)
        grad_own = grads[0]
    (joint_grad,) = call(
        last_kernel,
        [
            place_ref,
            down,
            right,
            *grads,
            projected,
            joint,
            grad_rows,
            grad_projected,
            normed,
            mixed,
        ],
        [((WIDTH, JOINT), bf16)],
        [held],
        2 * layer_flops,
        2 * layer_bytes,
    )
    reduced = lax.psum_scatter(joint_grad, "dp", scatter_dimension=0, tiled=True)
    qkv_grad = reduced[:, :QKV].astype(f32)
    proj_grad = reduced[:, PROJ_AT:].T.astype(f32)

    activated, joint_grad = lax.optimization_barrier((activated, joint_grad))
    visual_terms = jnp.einsum(
        "tr,rjf->jtf",
        activated,
        merge_out.reshape(HIDDEN, 16, FEATURES),
        preferred_element_type=f32,
    ).astype(bf16)
    visual = lax.all_to_all(visual_terms, ("section", "mp"), 0, 0)
    visual = jnp.sum(visual.astype(f32), axis=0).astype(bf16).reshape(2, MERGED, FEATURES)
    placed = jnp.einsum("mts,mtf->msf", chosen_bf, visual, preferred_element_type=f32)
    taken = jnp.any(chosen, axis=1)[:, :, None]
    joined = jnp.where(taken, placed.astype(bf16), text_embeds)
    merge_out_grad = merger_grad[:, :FEATURES].astype(f32)
    merge_in_grad = merger_grad[:, FEATURES:].astype(f32)
    return (joined, qkv_grad[None], proj_grad[None], merge_in_grad, merge_out_grad)


def solution(mesh):
    return jax.shard_map(
        local,
        mesh=mesh,
        in_specs=(
            P(None, "dp", None),
            P(None, "dp", None),
            P(None, "dp"),
            P(None, "dp", None),
            P("section", "dp", "mp"),
            P("section", "mp", "dp"),
            P(None, ("section", "mp")),
            P(("section", "mp"), None),
            P(None, "dp", ("section", "mp")),
            P(None, "dp", ("section", "mp")),
        ),
        out_specs=(
            P(None, "dp", ("section", "mp")),
            P("section", "dp", "mp"),
            P("section", "mp", "dp"),
            P("dp", ("section", "mp")),
            P(("section", "mp"), "dp"),
        ),
        check_vma=False,
    )
```

profile of v0, /device:TPU:6, one launch (start us, length us, event | category | flops | bytes accessed | tf_op | source)
XLA Modules:
  0.0 444.7 jit_solution(6914641753929643013)
XLA Ops:
  14.4 24.2 %all_gather.6.visual_grad = bf16[16,48,512]{2,1,0:T(8,128)(2,1)S(1)} all-gather(bf16[1,48,512]{2,1,0:T(8,128)(2,1)S(1)} %bitcast.119), channel_id=1, replica_groups=mesh['dp'=16,'section'=4,'mp'=4] {'section','mp'}, dimensions={0}, use_global_device_ids=true | all-gather | bytes 835584 | tf_op jit(solution)/shard_map/all_gather | solution.py:319
  38.7 4.8 %fusion.13.grad_act = f32[48,320]{1,0:T(8,128)} fusion(bf16[16,48,512]{2,1,0:T(8,128)(2,1)S(1)} %all_gather.6.visual_grad, bf16[40,16,8,512]{3,2,1,0:T(8,128)(2,1)} %bitcast.111), kind=kOutput, calls=%fused_computation.10 | convolution fusion | flops 251658240 | bytes 6090752 | tf_op jit(solution)/shard_map/jtf,rjf->tr/dot_general | solution.py:320
  43.5 11.4 %all-gather.2.cloned.1.call-done.weight = bf16[1280,1344]{1,0:T(8,128)(2,1)} async-done(((bf16[80,1344]{1,0:T(8,128)(2,1)}), bf16[1280,1344]{1,0:T(8,128)(2,1)}) %all-gather.2.cloned.1.call-update) | async-done | bytes 3440656 | tf_op jit(solution)/shard_map/all_gather | solution.py:296
  56.9 3.1 shard_map.137
  60.1 4.3 all-to-all-start
  64.4 9.5 %all-to-all-done = bf16[4,48,1280]{2,1,0:T(8,128)(2,1)S(1)} async-done(((bf16[4,48,1280]{2,1,0:T(8,128)(2,1)}), bf16[4,48,1280]{2,1,0:T(8,128)(2,1)S(1)}, u32[]{:S(2)}, u32[]{:S(2)}) %all-to-all-start) | async-done | bytes 491552 | tf_op jit(solution)/shard_map/all_to_all | solution.py:51
  81.2 11.1 %all_to_all.55 = bf16[4,48,1280]{2,1,0:T(8,128)(2,1)S(1)} all-to-all(bf16[4,48,1280]{2,1,0:T(8,128)(2,1)S(1)} %shard_map.138), channel_id=1, replica_groups=mesh['dp'=16,'section'=4,'mp'=4] {'mp'}, dimensions={0} | all-to-all | bytes 983040 | tf_op jit(solution)/shard_map/all_to_all | solution.py:51
  97.5 10.3 %all_to_all.56 = bf16[4,48,1280]{2,1,0:T(8,128)(2,1)S(1)} all-to-all(bf16[4,48,1280]{2,1,0:T(8,128)(2,1)S(1)} %shard_map.139), channel_id=1, replica_groups=mesh['dp'=16,'section'=4,'mp'=4] {'mp'}, dimensions={0} | all-to-all | bytes 983040 | tf_op jit(solution)/shard_map/all_to_all | solution.py:51
  113.1 21.6 %collective-permute-done.11.x3 = bf16[48,1280]{1,0:T(8,128)(2,1)S(1)} collective-permute-done((bf16[48,1280]{1,0:T(8,128)(2,1)S(1)}, bf16[48,1280]{1,0:T(8,128)(2,1)S(1)}, u32[]{:S(2)}, u32[]{:S(2)}) %collective-permute-start.11) | collective-permute-done | bytes 122912 | tf_op jit(solution)/shard_map/ppermute | solution.py:36
  138.4 2.4 shard_map.140
  140.8 10.6 %all_to_all.57 = bf16[4,48,1280]{2,1,0:T(8,128)(2,1)S(1)} all-to-all(bf16[4,48,1280]{2,1,0:T(8,128)(2,1)S(1)} %shard_map.140), channel_id=1, replica_groups=mesh['dp'=16,'section'=4,'mp'=4] {'mp'}, dimensions={0} | all-to-all | bytes 983040 | tf_op jit(solution)/shard_map/all_to_all | solution.py:51
  158.8 3.5 all-to-all-start.4
  162.3 5.8 %copy.52.weight = bf16[5120,320]{1,0:T(8,128)(2,1)} copy(bf16[5120,320]{0,1:T(8,128)(2,1)} %param.16) | data formatting | bytes 6553600 | tf_op args[6]
  173.1 3.0 shard_map.141
  176.7 4.1 all-to-all-start.5
  186.0 2.9 all-to-all-done.5
  197.8 5.5 %shard_map.143 = bf16[16,320,832]{2,1,0:T(8,128)(2,1)S(1)} custom-call(bf16[16,48,320]{2,1,0:T(8,128)(2,1)S(1)} %bitcast.110, bf16[48,320]{1,0:T(8,128)(2,1)S(1)} %copy-done.15, bf16[48,320]{1,0:T(8,128)(2,1)S(1)} %get-tuple-element.57.activated, bf16[16,48,512]{2,1,0:T(8,128)(2,1)S(1)} %all_gather.6.visual_grad), custom_call_target="tpu_custom_call" | custom-call | flops 408944640 | bytes 17039360 | tf_op jit(solution)/shard_map/pallas_call | solution.py:240
  203.3 3.5 copy-done.5
  209.3 10.3 %all_to_all.58 = bf16[4,48,1280]{2,1,0:T(8,128)(2,1)S(1)} all-to-all(bf16[4,48,1280]{2,1,0:T(8,128)(2,1)S(1)} %broadcast_in_dim.136), channel_id=1, replica_groups=mesh['dp'=16,'section'=4,'mp'=4] {'mp'}, dimensions={0} | all-to-all | bytes 983040 | tf_op jit(solution)/shard_map/all_to_all | solution.py:51
  219.7 3.5 shard_map.144
  223.3 10.3 %all_to_all.59 = bf16[4,48,1280]{2,1,0:T(8,128)(2,1)S(1)} all-to-all(bf16[4,48,1280]{2,1,0:T(8,128)(2,1)S(1)} %get-tuple-element.46), channel_id=1, replica_groups=mesh['dp'=16,'section'=4,'mp'=4] {'mp'}, dimensions={0} | all-to-all | bytes 983040 | tf_op jit(solution)/shard_map/all_to_all | solution.py:51
  233.9 6.7 %collective-permute-start.21 = (bf16[48,1280]{1,0:T(8,128)(2,1)S(1)}, bf16[48,1280]{1,0:T(8,128)(2,1)S(1)}, u32[]{:S(2)}, u32[]{:S(2)}) collective-permute-start(bf16[48,1280]{1,0:T(8,128)(2,1)S(1)} %fusion.25), channel_id=1, source_target_pairs={{12,11},{13,8},{14,9},{15,10},{28,27},{29,24},{30,25},{31,26},{44,... | collective-permute-start | bytes 368648 | tf_op jit(solution)/shard_map/ppermute | solution.py:36
  247.4 3.6 shard_map.145
  250.9 14.6 %all_to_all.60 = bf16[4,48,1280]{2,1,0:T(8,128)(2,1)S(1)} all-to-all(bf16[4,48,1280]{2,1,0:T(8,128)(2,1)S(1)} %get-tuple-element.49), channel_id=1, replica_groups=mesh['dp'=16,'section'=4,'mp'=4] {'mp'}, dimensions={0} | all-to-all | bytes 983040 | tf_op jit(solution)/shard_map/all_to_all | solution.py:51
  268.8 3.6 shard_map.146
  272.4 10.3 %all_to_all.61 = bf16[4,48,1280]{2,1,0:T(8,128)(2,1)S(1)} all-to-all(bf16[4,48,1280]{2,1,0:T(8,128)(2,1)S(1)} %get-tuple-element.52), channel_id=1, replica_groups=mesh['dp'=16,'section'=4,'mp'=4] {'mp'}, dimensions={0} | all-to-all | bytes 983040 | tf_op jit(solution)/shard_map/all_to_all | solution.py:51
  285.8 3.9 shard_map.147
  292.3 4.6 %fusion.9 = bf16[16,48,512]{2,1,0:T(8,128)(2,1)} fusion(bf16[40,16,8,512]{3,2,1,0:T(8,128)(2,1)} %bitcast.112, bf16[48,320]{1,0:T(8,128)(2,1)S(1)} %get-tuple-element.57.activated), kind=kOutput, calls=%fused_computation.7 | convolution fusion | flops 252051456 | bytes 6060032 | tf_op jit(solution)/shard_map/tr,rjf->jtf/dot_general | solution.py:437
  296.9 17.0 %all-to-all-start.10 = ((bf16[16,48,512]{2,1,0:T(8,128)(2,1)}), bf16[16,48,512]{2,1,0:T(8,128)(2,1)S(1)}, u32[]{:S(2)}, u32[]{:S(2)}) async-start(bf16[16,48,512]{2,1,0:T(8,128)(2,1)} %fusion.9), calls=%async_computation.10 | async-start | bytes 1572864 | tf_op jit(solution)/shard_map/all_to_all | solution.py:443
  314.0 9.3 %all-to-all-done.10 = bf16[16,48,512]{2,1,0:T(8,128)(2,1)S(1)} async-done(((bf16[16,48,512]{2,1,0:T(8,128)(2,1)}), bf16[16,48,512]{2,1,0:T(8,128)(2,1)S(1)}, u32[]{:S(2)}, u32[]{:S(2)}) %all-to-all-start.10) | async-done | bytes 786464 | tf_op jit(solution)/shard_map/all_to_all | solution.py:443
  324.6 36.8 %reduce-scatter.3.cloned.1.call-done = bf16[80,1344]{1,0:T(8,128)(2,1)} async-done(((bf16[1280,1344]{1,0:T(8,128)(2,1)}), bf16[80,1344]{1,0:T(8,128)(2,1)}) %reduce-scatter.3.cloned.1.call-update) | async-done | bytes 215056 | tf_op jit(solution)/shard_map/reduce_scatter | solution.py:432
  364.6 69.9 %reduce-scatter.5.cloned.1.call-done = bf16[1,320,832]{2,1,0:T(8,128)(2,1)} async-done(((bf16[16,320,832]{2,1,0:T(8,128)(2,1)}), bf16[1,320,832]{2,1,0:T(8,128)(2,1)}) %reduce-scatter.5.cloned.1.call-update) | async-done | bytes 532496 | tf_op jit(solution)/shard_map/reduce_scatter | solution.py:390
  (172 shorter events, 84.0 us)
Async XLA Ops:
  7.2 47.7 %all-gather.2.cloned.1.call-start = ((), (), s32[]{:S(2)}) async-start(), calls=%async_computation.13 | async-start | bytes 3829760 | tf_op jit(solution)/shard_map/all_gather | solution.py:296
  60.1 13.8 %all-to-all-start = ((bf16[4,48,1280]{2,1,0:T(8,128)(2,1)}), bf16[4,48,1280]{2,1,0:T(8,128)(2,1)S(1)}, u32[]{:S(2)}, u32[]{:S(2)}) async-start(bf16[4,48,1280]{2,1,0:T(8,128)(2,1)} %shard_map.137), calls=%async_computation | async-start | bytes 983040 | tf_op jit(solution)/shard_map/all_to_all | solution.py:51
  74.0 2.7 collective-permute-start.3
  74.7 2.0 collective-permute-start.2
  92.4 2.7 collective-permute-start.7
  93.1 2.0 collective-permute-start.6
  93.7 1.4 collective-permute-start.5
  107.9 26.8 %collective-permute-start.11 = (bf16[48,1280]{1,0:T(8,128)(2,1)S(1)}, bf16[48,1280]{1,0:T(8,128)(2,1)S(1)}, u32[]{:S(2)}, u32[]{:S(2)}) collective-permute-start(bf16[48,1280]{1,0:T(8,128)(2,1)S(1)} %add_convert_fusion.1), channel_id=1, source_target_pairs={{8,15},{9,12},{10,13},{11,14},{24,31},{25,28},{26,29},{27,30},{40,... | collective-permute-start | bytes 368648 | tf_op jit(solution)/shard_map/ppermute | solution.py:36
  109.2 26.9 %collective-permute-start.10 = (bf16[48,1280]{1,0:T(8,128)(2,1)S(1)}, bf16[48,1280]{1,0:T(8,128)(2,1)S(1)}, u32[]{:S(2)}, u32[]{:S(2)}) collective-permute-start(bf16[48,1280]{1,0:T(8,128)(2,1)S(1)} %add_convert_fusion.1), channel_id=1, source_target_pairs={{8,14},{9,15},{10,12},{11,13},{24,30},{25,31},{26,28},{27,29},{40,... | collective-permute-start | bytes 368648 | tf_op jit(solution)/shard_map/ppermute | solution.py:36
  110.5 27.2 %collective-permute-start.9 = (bf16[48,1280]{1,0:T(8,128)(2,1)S(1)}, bf16[48,1280]{1,0:T(8,128)(2,1)S(1)}, u32[]{:S(2)}, u32[]{:S(2)}) collective-permute-start(bf16[48,1280]{1,0:T(8,128)(2,1)S(1)} %add_convert_fusion.1), channel_id=1, source_target_pairs={{8,13},{9,14},{10,15},{11,12},{24,29},{25,30},{26,31},{27,28},{40,... | collective-permute-start | bytes 368648 | tf_op jit(solution)/shard_map/ppermute | solution.py:36
  111.8 26.6 %collective-permute-start.8 = (bf16[48,1280]{1,0:T(8,128)(2,1)S(1)}, bf16[48,1280]{1,0:T(8,128)(2,1)S(1)}, u32[]{:S(2)}, u32[]{:S(2)}) collective-permute-start(bf16[48,1280]{1,0:T(8,128)(2,1)S(1)} %add_convert_fusion.1), channel_id=1, source_target_pairs={{8,12},{9,13},{10,14},{11,15},{24,28},{25,29},{26,30},{27,31},{40,... | collective-permute-start | bytes 368648 | tf_op jit(solution)/shard_map/ppermute | solution.py:36
  151.6 3.9 collective-permute-start.14
  152.9 3.7 collective-permute-start.13
  154.2 3.7 collective-permute-start.12
  158.8 11.3 %all-to-all-start.4 = ((bf16[4,48,1280]{2,1,0:T(8,128)(2,1)}), bf16[4,48,1280]{2,1,0:T(8,128)(2,1)S(1)}, u32[]{:S(2)}, u32[]{:S(2)}) async-start(bf16[4,48,1280]{2,1,0:T(8,128)(2,1)} %broadcast_in_dim.134), calls=%async_computation.4 | async-start | bytes 983040 | tf_op jit(solution)/shard_map/all_to_all | solution.py:51
  176.7 12.1 %all-to-all-start.5 = ((bf16[4,48,1280]{2,1,0:T(8,128)(2,1)}), bf16[4,48,1280]{2,1,0:T(8,128)(2,1)}, u32[]{:S(2)}, u32[]{:S(2)}) async-start(bf16[4,48,1280]{2,1,0:T(8,128)(2,1)} %get-tuple-element.35), calls=%async_computation.5 | async-start | bytes 983040 | tf_op jit(solution)/shard_map/all_to_all | solution.py:51
  180.9 180.6 %reduce-scatter.3.cloned.1.call-start = ((), (), s32[]{:S(2)}) async-start(), calls=%async_computation.14 | async-start | bytes 3829760 | tf_op jit(solution)/shard_map/reduce_scatter | solution.py:432
  190.6 16.2 %collective-permute-start.17 = (bf16[48,1280]{1,0:T(8,128)(2,1)}, bf16[48,1280]{1,0:T(8,128)(2,1)S(1)}, u32[]{:S(2)}, u32[]{:S(2)}) collective-permute-start(bf16[48,1280]{1,0:T(8,128)(2,1)} %convert_element_type.142), channel_id=1, source_target_pairs={{8,12},{9,13},{10,14},{11,15},{24,28},{25,29},{26,30},{27,31},{40,... | collective-permute-start | bytes 368648 | tf_op jit(solution)/shard_map/ppermute | solution.py:36
  191.9 14.9 %collective-permute-start.16 = (bf16[48,1280]{1,0:T(8,128)(2,1)}, bf16[48,1280]{1,0:T(8,128)(2,1)}, u32[]{:S(2)}, u32[]{:S(2)}) collective-permute-start(bf16[48,1280]{1,0:T(8,128)(2,1)} %convert_element_type.142), channel_id=1, source_target_pairs={{4,12},{5,13},{6,14},{7,15},{20,28},{21,29},{22,30},{23,31},{36,44... | collective-permute-start | bytes 368648 | tf_op jit(solution)/shard_map/ppermute | solution.py:36
  193.2 13.6 %collective-permute-start.15 = (bf16[48,1280]{1,0:T(8,128)(2,1)}, bf16[48,1280]{1,0:T(8,128)(2,1)}, u32[]{:S(2)}, u32[]{:S(2)}) collective-permute-start(bf16[48,1280]{1,0:T(8,128)(2,1)} %convert_element_type.142), channel_id=1, source_target_pairs={{0,12},{1,13},{2,14},{3,15},{16,28},{17,29},{18,30},{19,31},{32,44... | collective-permute-start | bytes 368648 | tf_op jit(solution)/shard_map/ppermute | solution.py:36
  233.9 11.0 %collective-permute-start.21 = (bf16[48,1280]{1,0:T(8,128)(2,1)S(1)}, bf16[48,1280]{1,0:T(8,128)(2,1)S(1)}, u32[]{:S(2)}, u32[]{:S(2)}) collective-permute-start(bf16[48,1280]{1,0:T(8,128)(2,1)S(1)} %fusion.25), channel_id=1, source_target_pairs={{12,11},{13,8},{14,9},{15,10},{28,27},{29,24},{30,25},{31,26},{44,... | collective-permute-start | bytes 368648 | tf_op jit(solution)/shard_map/ppermute | solution.py:36
  240.6 4.3 collective-permute-start.20
  242.3 3.7 collective-permute-start.19
  243.6 3.7 collective-permute-start.18
  265.9 2.9 collective-permute-start.25
  266.5 2.3 collective-permute-start.24
  267.2 1.6 collective-permute-start.23
  283.1 2.7 collective-permute-start.29
  283.7 2.0 collective-permute-start.28
  284.4 1.4 collective-permute-start.27
  291.6 143.0 %reduce-scatter.5.cloned.1.call-start = ((), (), s32[]{:S(2)}) async-start(), calls=%async_computation.15 | async-start | bytes 9748480 | tf_op jit(solution)/shard_map/reduce_scatter | solution.py:390
  296.9 26.4 %all-to-all-start.10 = ((bf16[16,48,512]{2,1,0:T(8,128)(2,1)}), bf16[16,48,512]{2,1,0:T(8,128)(2,1)S(1)}, u32[]{:S(2)}, u32[]{:S(2)}) async-start(bf16[16,48,512]{2,1,0:T(8,128)(2,1)} %fusion.9), calls=%async_computation.10 | async-start | bytes 1572864 | tf_op jit(solution)/shard_map/all_to_all | solution.py:443
  (25 other events, 233.7 us)
Sparse Core Ops, SparseCore 0:
  10.4 44.4 all-gather.1
  291.7 69.7 reduce-scatter.2
  364.0 70.4 reduce-scatter.4
where the time goes:
time: 447 us; the launch traced here: 445 us
  waiting for transfers between devices  173 us (39%)
  blocking collectives  102 us (23%)
  starting transfers between devices  63.8 us (14%)
  Pallas kernels  35.1 us (8%)
  local copies, waits for them, and re-layouts  30.3 us (7%)
  other arithmetic  15.7 us (4%)
  between operations  14.6 us (3%)
  matrix products  10.8 us (2%)
    all_to_all x7, blocking collectives, exchange(): return lax.all_to_all(value, 'mp', 0, 0)  77.4 us
    reduce_scatter x1, waiting for transfers between devices, local(): lax.psum_scatter(merger_grad, 'dp', scatter_dimension=0, tiled=False)  69.9 us
    reduce_scatter x1, waiting for transfers between devices, local(): lax.psum_scatter(joint_grad, 'dp', scatter_dimension=0, tiled=True)  36.8 us
    ppermute x30, starting transfers between devices, permute(): return lax.ppermute(value, ('section', 'mp'), pairs)  34.8 us
    ppermute x30, waiting for transfers between devices, permute(): return lax.ppermute(value, ('section', 'mp'), pairs)  30.1 us
    pallas_call x10, Pallas kernels, call(): pl.pallas_call(kernel, in_specs=[pl.BlockSpec(memory_space=pltpu.SMEM)] +...  29.6 us
    all_gather x1, blocking collectives, local(): visual_grad_full = lax.all_gather(visual_grad, ('section', 'mp'), axis=0)  24.2 us
    unnamed x41, local copies, waits for them, and re-layouts  21.6 us
  transfers between devices with their start and end apart: 37, of which 15 were waited for; matrix products, arithmetic and copies ran while one was open for 7% of the time, Pallas kernels for 2%

commit v1 on v0

--- a/solution.py
+++ b/solution.py
@@ -218,8 +218,9 @@
     for quarter in range(QUARTERS):
         at = slice(quarter * WIDTH, (quarter + 1) * WIDTH)
         normed = unit_rows(blocks[quarter].astype(f32)).astype(bf16)
-        merged[:, at] = normed
-        before = before + dot(normed, weight[at, :])
+        for part_at in range(4):
+            merged[4 * quarter + part_at] = normed[:, HIDDEN * part_at : HIDDEN * (part_at + 1)]
+        before = before + dot_nt(normed, weight[:, at])
     tail = 0.5 * (1.0 + lax.erf(before * math.sqrt(0.5)))
     bell = jnp.exp(-0.5 * before * before) * (1.0 / math.sqrt(2.0 * math.pi))
     activated[...] = (before * tail).astype(bf16)
@@ -227,7 +228,7 @@
     grad_before[...] = grad
     for quarter in range(QUARTERS):
         at = slice(quarter * WIDTH, (quarter + 1) * WIDTH)
-        part[quarter] = dot_nt(grad, weight[at, :]).astype(bf16)
+        part[quarter] = dot(grad, weight[:, at]).astype(bf16)
 
 
 def merger_grad_kernel(merged, grad_before, activated, visual_grad, out):
@@ -360,9 +361,9 @@
     own = jnp.where(is_last, own, sent[0] + sent[1] + sent[2])
     merged, activated, grad_before, terms = call(
         merge_kernel,
-        [place_ref, everyones(own), merge_in, grad_act],
+        [place_ref, everyones(own), merge_in.T, grad_act],
         [
-            ((TOKENS, QUARTERS * WIDTH), bf16),
+            ((16, TOKENS, HIDDEN), bf16),
             ((TOKENS, HIDDEN), bf16),
             ((TOKENS, HIDDEN), bf16),
             PART,
@@ -382,12 +383,7 @@
 
     total = jnp.sum(exchange(terms).astype(f32), axis=0)
     leaving = total.astype(bf16)
-    leaving, merged, normed = lax.optimization_barrier((leaving, merged, normed))
     arrived = [permute(leaving, across(s, SECTIONS - 1)) for s in range(SECTIONS - 1)]
-    merged = jnp.swapaxes(merged.reshape(TOKENS, 16, HIDDEN), 0, 1)
-    merger_grad = merger_grads(merged, grad_before, activated, visual_grad_full)
-    *arrived, merger_grad = lax.optimization_barrier((*arrived, merger_grad))
-    merger_grad = lax.psum_scatter(merger_grad, "dp", scatter_dimension=0, tiled=False)
     for term in arrived:
         total = total + term.astype(f32)
     grad_own = unit_back(own.astype(f32), total)
@@ -408,7 +404,16 @@
         )
         total = jnp.sum(exchange(terms).astype(f32), axis=0)
         grad_own = grad_own.astype(f32) + unit_back(saved[0].astype(f32), total)
-        grads = to_section(grad_own.astype(bf16), layer, layer - 1)
+        grad_own = grad_own.astype(bf16)
+        if layer == SECTIONS - 1:
+            merged, grad_own = lax.optimization_barrier((merged, grad_own))
+            merger_grad = merger_grads(merged, grad_before, activated, visual_grad_full)
+        grads = to_section(grad_own, layer, layer - 1)
+        if layer == SECTIONS - 1:
+            place_ref, merger_grad = lax.optimization_barrier((place_ref, merger_grad))
+            merger_grad = lax.psum_scatter(
+                merger_grad, "dp", scatter_dimension=0, tiled=False
+            )
         grad_own = grads[0]
     (joint_grad,) = call(
         last_kernel,
@@ -429,6 +434,7 @@
         2 * layer_flops,
         2 * layer_bytes,
     )
+    joint_grad, merger_grad = lax.optimization_barrier((joint_grad, merger_grad))
     reduced = lax.psum_scatter(joint_grad, "dp", scatter_dimension=0, tiled=True)
     qkv_grad = reduced[:, :QKV].astype(f32)
     proj_grad = reduced[:, PROJ_AT:].T.astype(f32)

time: 447 us -> 382 us (0.85)
  waiting for transfers between devices: 173 us -> 128 us
  starting transfers between devices: 63.8 us -> 44.8 us
  blocking collectives: 102 us -> 109 us
  local copies, waits for them, and re-layouts: 30.3 us -> 25.6 us
    reduce_scatter x1, waiting for transfers between devices: 69.9 us -> 17.9 us  [local(): lax.psum_scatter(merger_grad, 'dp', scatter_dimension=0, tiled=False)]
    all_to_all x1, starting transfers between devices: 17 us -> 7.02 us  [local(): visual = lax.all_to_all(visual_terms, ('section', 'mp'), 0, 0)]
    ppermute x30, waiting for transfers between devices: 30.1 us -> 37.4 us  [permute(): return lax.ppermute(value, ('section', 'mp'), pairs)]
    all_to_all x7 -> x8, blocking collectives: 77.4 us -> 84.3 us  [exchange(): return lax.all_to_all(value, 'mp', 0, 0)]
    ppermute x30, starting transfers between devices: 34.8 us -> 29.3 us  [permute(): return lax.ppermute(value, ('section', 'mp'), pairs)]
    all_to_all x3 -> x2, starting transfers between devices: 11.9 us -> 8.4 us  [exchange(): return lax.all_to_all(value, 'mp', 0, 0)]
    unnamed x41 -> x48, local copies, waits for them, and re-layouts: 21.6 us -> 18.3 us
    all_to_all x3 -> x2, waiting for transfers between devices: 14.4 us -> 11.9 us  [exchange(): return lax.all_to_all(value, 'mp', 0, 0)]
  transfers between devices with their start and end apart: 37 -> 36, of which waited for: 15 -> 17; matrix products, arithmetic and copies ran while one was open for 7% -> 5% of each run, Pallas kernels for 2% -> 3%
where the time goes in v1:
time: 382 us; the launch traced here: 380 us
  waiting for transfers between devices  128 us (34%)
  blocking collectives  109 us (29%)
  starting transfers between devices  44.8 us (12%)
  Pallas kernels  34.7 us (9%)
  local copies, waits for them, and re-layouts  25.6 us (7%)
  between operations  14.6 us (4%)
  other arithmetic  13.5 us (4%)
  matrix products  10.7 us (3%)
    all_to_all x8, blocking collectives, exchange(): return lax.all_to_all(value, 'mp', 0, 0)  84.3 us
    reduce_scatter x1, waiting for transfers between devices, local(): lax.psum_scatter(joint_grad, 'dp', scatter_dimension=0, tiled=True)  41 us
    ppermute x30, waiting for transfers between devices, permute(): return lax.ppermute(value, ('section', 'mp'), pairs)  37.4 us
    ppermute x30, starting transfers between devices, permute(): return lax.ppermute(value, ('section', 'mp'), pairs)  29.3 us
    pallas_call x10, Pallas kernels, call(): pl.pallas_call(kernel, in_specs=[pl.BlockSpec(memory_space=pltpu.SMEM)] +...  29.2 us
    all_gather x1, blocking collectives, local(): visual_grad_full = lax.all_gather(visual_grad, ('section', 'mp'), axis=0)  24.2 us
    unnamed x48, local copies, waits for them, and re-layouts  18.3 us
    reduce_scatter x1, waiting for transfers between devices, local(): lax.psum_scatter(merger_grad, 'dp', scatter_dimension=0, tiled=False)  17.9 us
  transfers between devices with their start and end apart: 36, of which 17 were waited for; matrix products, arithmetic and copies ran while one was open for 5% of the time, Pallas kernels for 3%

profile of v1, /device:TPU:6, one launch (start us, length us, event | category | flops | bytes accessed | tf_op | source)
XLA Modules:
  0.0 380.0 jit_solution(11492343677168594998)
XLA Ops:
  14.4 24.2 %all_gather.6.visual_grad = bf16[16,48,512]{2,1,0:T(8,128)(2,1)S(1)} all-gather(bf16[1,48,512]{2,1,0:T(8,128)(2,1)S(1)} %bitcast.117), channel_id=1, replica_groups=mesh['dp'=16,'section'=4,'mp'=4] {'section','mp'}, dimensions={0}, use_global_device_ids=true | all-gather | bytes 835584 | tf_op jit(solution)/shard_map/all_gather | solution.py:320
  38.7 4.8 %fusion.13.grad_act = f32[48,320]{1,0:T(8,128)} fusion(bf16[16,48,512]{2,1,0:T(8,128)(2,1)S(1)} %all_gather.6.visual_grad, bf16[40,16,8,512]{3,2,1,0:T(8,128)(2,1)} %bitcast.109), kind=kOutput, calls=%fused_computation.10 | convolution fusion | flops 251658240 | bytes 6090752 | tf_op jit(solution)/shard_map/jtf,rjf->tr/dot_general | solution.py:321
  43.5 11.4 %all-gather.2.cloned.1.call-done.weight = bf16[1280,1344]{1,0:T(8,128)(2,1)} async-done(((bf16[80,1344]{1,0:T(8,128)(2,1)}), bf16[1280,1344]{1,0:T(8,128)(2,1)}) %all-gather.2.cloned.1.call-update) | async-done | bytes 3440656 | tf_op jit(solution)/shard_map/all_gather | solution.py:297
  56.9 3.1 shard_map.137
  60.1 4.3 %all-to-all-start = ((bf16[4,48,1280]{2,1,0:T(8,128)(2,1)}), bf16[4,48,1280]{2,1,0:T(8,128)(2,1)S(1)}, u32[]{:S(2)}, u32[]{:S(2)}) async-start(bf16[4,48,1280]{2,1,0:T(8,128)(2,1)} %shard_map.137), calls=%async_computation | async-start | bytes 983040 | tf_op jit(solution)/shard_map/all_to_all | solution.py:51
  64.4 9.5 %all-to-all-done = bf16[4,48,1280]{2,1,0:T(8,128)(2,1)S(1)} async-done(((bf16[4,48,1280]{2,1,0:T(8,128)(2,1)}), bf16[4,48,1280]{2,1,0:T(8,128)(2,1)S(1)}, u32[]{:S(2)}, u32[]{:S(2)}) %all-to-all-start) | async-done | bytes 491552 | tf_op jit(solution)/shard_map/all_to_all | solution.py:51
  78.8 2.4 shard_map.138
  81.2 11.1 %all_to_all.55 = bf16[4,48,1280]{2,1,0:T(8,128)(2,1)S(1)} all-to-all(bf16[4,48,1280]{2,1,0:T(8,128)(2,1)S(1)} %shard_map.138), channel_id=1, replica_groups=mesh['dp'=16,'section'=4,'mp'=4] {'mp'}, dimensions={0} | all-to-all | bytes 983040 | tf_op jit(solution)/shard_map/all_to_all | solution.py:51
  95.1 2.4 shard_map.139
  97.5 10.3 %all_to_all.56 = bf16[4,48,1280]{2,1,0:T(8,128)(2,1)S(1)} all-to-all(bf16[4,48,1280]{2,1,0:T(8,128)(2,1)S(1)} %shard_map.139), channel_id=1, replica_groups=mesh['dp'=16,'section'=4,'mp'=4] {'mp'}, dimensions={0} | all-to-all | bytes 983040 | tf_op jit(solution)/shard_map/all_to_all | solution.py:51
  113.4 21.6 %collective-permute-done.11.x3 = bf16[48,1280]{1,0:T(8,128)(2,1)S(1)} collective-permute-done((bf16[48,1280]{1,0:T(8,128)(2,1)S(1)}, bf16[48,1280]{1,0:T(8,128)(2,1)S(1)}, u32[]{:S(2)}, u32[]{:S(2)}) %collective-permute-start.11) | collective-permute-done | bytes 122912 | tf_op jit(solution)/shard_map/ppermute | solution.py:36
  141.1 10.6 %all_to_all.57 = bf16[4,48,1280]{2,1,0:T(8,128)(2,1)S(1)} all-to-all(bf16[4,48,1280]{2,1,0:T(8,128)(2,1)S(1)} %shard_map.140), channel_id=1, replica_groups=mesh['dp'=16,'section'=4,'mp'=4] {'mp'}, dimensions={0} | all-to-all | bytes 983040 | tf_op jit(solution)/shard_map/all_to_all | solution.py:51
  158.3 10.5 %all_to_all.58.blocks = bf16[4,48,1280]{2,1,0:T(8,128)(2,1)S(1)} all-to-all(bf16[4,48,1280]{2,1,0:T(8,128)(2,1)S(1)} %broadcast_in_dim.134), channel_id=1, replica_groups=mesh['dp'=16,'section'=4,'mp'=4] {'mp'}, dimensions={0} | all-to-all | bytes 983040 | tf_op jit(solution)/shard_map/all_to_all | solution.py:51
  168.7 2.6 shard_map.141
  171.4 10.3 %all_to_all.59 = bf16[4,48,1280]{2,1,0:T(8,128)(2,1)S(1)} all-to-all(bf16[4,48,1280]{2,1,0:T(8,128)(2,1)S(1)} %get-tuple-element.35), channel_id=1, replica_groups=mesh['dp'=16,'section'=4,'mp'=4] {'mp'}, dimensions={0} | all-to-all | bytes 983040 | tf_op jit(solution)/shard_map/all_to_all | solution.py:51
  187.0 3.1 collective-permute-done.17
  190.2 2.8 collective-permute-done.16
  198.4 4.1 %all-to-all-start.6 = ((bf16[4,48,1280]{2,1,0:T(8,128)(2,1)}), bf16[4,48,1280]{2,1,0:T(8,128)(2,1)}, u32[]{:S(2)}, u32[]{:S(2)}) async-start(bf16[4,48,1280]{2,1,0:T(8,128)(2,1)} %broadcast_in_dim.136), calls=%async_computation.6 | async-start | bytes 983040 | tf_op jit(solution)/shard_map/all_to_all | solution.py:51
  213.7 3.5 shard_map.143
  217.3 10.3 %all_to_all.60 = bf16[4,48,1280]{2,1,0:T(8,128)(2,1)S(1)} all-to-all(bf16[4,48,1280]{2,1,0:T(8,128)(2,1)S(1)} %get-tuple-element.37), channel_id=1, replica_groups=mesh['dp'=16,'section'=4,'mp'=4] {'mp'}, dimensions={0} | all-to-all | bytes 983040 | tf_op jit(solution)/shard_map/all_to_all | solution.py:51
  228.6 5.5 %shard_map.144 = bf16[16,320,832]{2,1,0:T(8,128)(2,1)S(1)} custom-call(bf16[16,48,320]{2,1,0:T(8,128)(2,1)S(1)} %get-tuple-element.38.merged, bf16[48,320]{1,0:T(8,128)(2,1)S(1)} %copy-done.16, bf16[48,320]{1,0:T(8,128)(2,1)S(1)} %get-tuple-element.55.activated, bf16[16,48,512]{2,1,0:T(8,128)(2,1)S(1)} %all_gather.6.visual_grad), custom_call_target="tpu_custom_call" | custom-call | flops 408944640 | bytes 17039360 | tf_op jit(solution)/shard_map/pallas_call | solution.py:241
  234.1 3.5 copy-done.6
  248.2 3.6 shard_map.145
  251.8 10.9 %all_to_all.61 = bf16[4,48,1280]{2,1,0:T(8,128)(2,1)S(1)} all-to-all(bf16[4,48,1280]{2,1,0:T(8,128)(2,1)S(1)} %get-tuple-element.45), channel_id=1, replica_groups=mesh['dp'=16,'section'=4,'mp'=4] {'mp'}, dimensions={0} | all-to-all | bytes 983040 | tf_op jit(solution)/shard_map/all_to_all | solution.py:51
  266.1 3.6 shard_map.146
  269.6 10.3 %all_to_all.62 = bf16[4,48,1280]{2,1,0:T(8,128)(2,1)S(1)} all-to-all(bf16[4,48,1280]{2,1,0:T(8,128)(2,1)S(1)} %get-tuple-element.48), channel_id=1, replica_groups=mesh['dp'=16,'section'=4,'mp'=4] {'mp'}, dimensions={0} | all-to-all | bytes 983040 | tf_op jit(solution)/shard_map/all_to_all | solution.py:51
  283.0 3.9 %shard_map.147 = bf16[1280,1344]{1,0:T(8,128)(2,1)S(1)} custom-call(s32[1]{0:T(128)} %bitcast.12.place_ref._, s32[192,1]{1,0:T(8,128)S(1)} %broadcast_in_dim_tile.8.down, s32[1,192]{1,0:T(1,128)S(1)} %broadcast_in_dim_tile.7.across_ref, bf16[48,1280]{1,0:T(8,128)(2,1)S(1)} %collective-permute-done.26.g0, bf16[48,1280]{1,0:T(8,128)(2,1)S(1)} %collective-permute-done.27.g1, ...), custom_call_target="tpu_custom_call" | custom-call | flops 1321205760 | bytes 10813440 | tf_op jit(solution)/shard_map/pallas_call | solution.py:262
  288.8 17.9 %reduce-scatter.3.cloned.1.call-done = bf16[1,320,832]{2,1,0:T(8,128)(2,1)} async-done(((bf16[16,320,832]{2,1,0:T(8,128)(2,1)}), bf16[1,320,832]{2,1,0:T(8,128)(2,1)}) %reduce-scatter.3.cloned.1.call-update) | async-done | bytes 532496 | tf_op jit(solution)/shard_map/reduce_scatter | solution.py:414
  306.7 4.5 %fusion.9 = bf16[16,48,512]{2,1,0:T(8,128)(2,1)} fusion(bf16[40,16,8,512]{3,2,1,0:T(8,128)(2,1)} %bitcast.110, bf16[48,320]{1,0:T(8,128)(2,1)S(1)} %get-tuple-element.55.activated), kind=kOutput, calls=%fused_computation.7 | convolution fusion | flops 252051456 | bytes 6060032 | tf_op jit(solution)/shard_map/tr,rjf->jtf/dot_general | solution.py:443
  311.2 7.0 %all-to-all-start.10 = ((bf16[16,48,512]{2,1,0:T(8,128)(2,1)}), bf16[16,48,512]{2,1,0:T(8,128)(2,1)S(1)}, u32[]{:S(2)}, u32[]{:S(2)}) async-start(bf16[16,48,512]{2,1,0:T(8,128)(2,1)} %fusion.9), calls=%async_computation.11 | async-start | bytes 1572864 | tf_op jit(solution)/shard_map/all_to_all | solution.py:449
  320.1 7.9 %all-to-all-done.10 = bf16[16,48,512]{2,1,0:T(8,128)(2,1)S(1)} async-done(((bf16[16,48,512]{2,1,0:T(8,128)(2,1)}), bf16[16,48,512]{2,1,0:T(8,128)(2,1)S(1)}, u32[]{:S(2)}, u32[]{:S(2)}) %all-to-all-start.10) | async-done | bytes 786464 | tf_op jit(solution)/shard_map/all_to_all | solution.py:449
  329.4 41.0 %reduce-scatter.5.cloned.1.call-done = bf16[80,1344]{1,0:T(8,128)(2,1)} async-done(((bf16[1280,1344]{1,0:T(8,128)(2,1)}), bf16[80,1344]{1,0:T(8,128)(2,1)}) %reduce-scatter.5.cloned.1.call-update) | async-done | bytes 215056 | tf_op jit(solution)/shard_map/reduce_scatter | solution.py:438
  (176 shorter events, 82.6 us)
Async XLA Ops:
  7.2 47.7 %all-gather.2.cloned.1.call-start = ((), (), s32[]{:S(2)}) async-start(), calls=%async_computation.13 | async-start | bytes 3829760 | tf_op jit(solution)/shard_map/all_gather | solution.py:297
  60.1 13.8 %all-to-all-start = ((bf16[4,48,1280]{2,1,0:T(8,128)(2,1)}), bf16[4,48,1280]{2,1,0:T(8,128)(2,1)S(1)}, u32[]{:S(2)}, u32[]{:S(2)}) async-start(bf16[4,48,1280]{2,1,0:T(8,128)(2,1)} %shard_map.137), calls=%async_computation | async-start | bytes 983040 | tf_op jit(solution)/shard_map/all_to_all | solution.py:51
  74.0 2.7 collective-permute-start.3
  74.7 2.0 collective-permute-start.2
  75.4 1.4 collective-permute-start.1
  92.4 2.7 collective-permute-start.7
  93.1 2.0 collective-permute-start.6
  93.7 1.4 collective-permute-start.5
  108.0 27.1 %collective-permute-start.11 = (bf16[48,1280]{1,0:T(8,128)(2,1)S(1)}, bf16[48,1280]{1,0:T(8,128)(2,1)S(1)}, u32[]{:S(2)}, u32[]{:S(2)}) collective-permute-start(bf16[48,1280]{1,0:T(8,128)(2,1)S(1)} %add_convert_fusion.1), channel_id=1, source_target_pairs={{8,15},{9,12},{10,13},{11,14},{24,31},{25,28},{26,29},{27,30},{40,... | collective-permute-start | bytes 368648 | tf_op jit(solution)/shard_map/ppermute | solution.py:36
  109.5 26.9 %collective-permute-start.10 = (bf16[48,1280]{1,0:T(8,128)(2,1)S(1)}, bf16[48,1280]{1,0:T(8,128)(2,1)S(1)}, u32[]{:S(2)}, u32[]{:S(2)}) collective-permute-start(bf16[48,1280]{1,0:T(8,128)(2,1)S(1)} %add_convert_fusion.1), channel_id=1, source_target_pairs={{8,14},{9,15},{10,12},{11,13},{24,30},{25,31},{26,28},{27,29},{40,... | collective-permute-start | bytes 368648 | tf_op jit(solution)/shard_map/ppermute | solution.py:36
  110.8 27.3 %collective-permute-start.9 = (bf16[48,1280]{1,0:T(8,128)(2,1)S(1)}, bf16[48,1280]{1,0:T(8,128)(2,1)S(1)}, u32[]{:S(2)}, u32[]{:S(2)}) collective-permute-start(bf16[48,1280]{1,0:T(8,128)(2,1)S(1)} %add_convert_fusion.1), channel_id=1, source_target_pairs={{8,13},{9,14},{10,15},{11,12},{24,29},{25,30},{26,31},{27,28},{40,... | collective-permute-start | bytes 368648 | tf_op jit(solution)/shard_map/ppermute | solution.py:36
  112.1 26.6 %collective-permute-start.8 = (bf16[48,1280]{1,0:T(8,128)(2,1)S(1)}, bf16[48,1280]{1,0:T(8,128)(2,1)S(1)}, u32[]{:S(2)}, u32[]{:S(2)}) collective-permute-start(bf16[48,1280]{1,0:T(8,128)(2,1)S(1)} %add_convert_fusion.1), channel_id=1, source_target_pairs={{8,12},{9,13},{10,14},{11,15},{24,28},{25,29},{26,30},{27,31},{40,... | collective-permute-start | bytes 368648 | tf_op jit(solution)/shard_map/ppermute | solution.py:36
  151.8 3.9 %collective-permute-start.14 = (bf16[48,1280]{1,0:T(8,128)(2,1)S(1)}, bf16[48,1280]{1,0:T(8,128)(2,1)S(1)}, u32[]{:S(2)}, u32[]{:S(2)}) collective-permute-start(bf16[48,1280]{1,0:T(8,128)(2,1)S(1)} %add_convert_fusion), channel_id=1, source_target_pairs={{12,8},{13,9},{14,10},{15,11},{28,24},{29,25},{30,26},{31,27},{44,... | collective-permute-start | bytes 368648 | tf_op jit(solution)/shard_map/ppermute | solution.py:36
  153.1 3.7 collective-permute-start.13
  154.4 3.7 collective-permute-start.12
  183.1 7.1 %collective-permute-start.17 = (bf16[48,1280]{1,0:T(8,128)(2,1)}, bf16[48,1280]{1,0:T(8,128)(2,1)}, u32[]{:S(2)}, u32[]{:S(2)}) collective-permute-start(bf16[48,1280]{1,0:T(8,128)(2,1)} %convert_element_type.142), channel_id=1, source_target_pairs={{8,12},{9,13},{10,14},{11,15},{24,28},{25,29},{26,30},{27,31},{40,... | collective-permute-start | bytes 368648 | tf_op jit(solution)/shard_map/ppermute | solution.py:36
  184.4 8.6 %collective-permute-start.16 = (bf16[48,1280]{1,0:T(8,128)(2,1)}, bf16[48,1280]{1,0:T(8,128)(2,1)}, u32[]{:S(2)}, u32[]{:S(2)}) collective-permute-start(bf16[48,1280]{1,0:T(8,128)(2,1)} %convert_element_type.142), channel_id=1, source_target_pairs={{4,12},{5,13},{6,14},{7,15},{20,28},{21,29},{22,30},{23,31},{36,44... | collective-permute-start | bytes 368648 | tf_op jit(solution)/shard_map/ppermute | solution.py:36
  185.7 8.6 %collective-permute-start.15 = (bf16[48,1280]{1,0:T(8,128)(2,1)}, bf16[48,1280]{1,0:T(8,128)(2,1)}, u32[]{:S(2)}, u32[]{:S(2)}) collective-permute-start(bf16[48,1280]{1,0:T(8,128)(2,1)} %convert_element_type.142), channel_id=1, source_target_pairs={{0,12},{1,13},{2,14},{3,15},{16,28},{17,29},{18,30},{19,31},{32,44... | collective-permute-start | bytes 368648 | tf_op jit(solution)/shard_map/ppermute | solution.py:36
  198.4 12.1 %all-to-all-start.6 = ((bf16[4,48,1280]{2,1,0:T(8,128)(2,1)}), bf16[4,48,1280]{2,1,0:T(8,128)(2,1)}, u32[]{:S(2)}, u32[]{:S(2)}) async-start(bf16[4,48,1280]{2,1,0:T(8,128)(2,1)} %broadcast_in_dim.136), calls=%async_computation.6 | async-start | bytes 983040 | tf_op jit(solution)/shard_map/all_to_all | solution.py:51
  202.5 104.2 %reduce-scatter.3.cloned.1.call-start = ((), (), s32[]{:S(2)}) async-start(), calls=%async_computation.14 | async-start | bytes 9748480 | tf_op jit(solution)/shard_map/reduce_scatter | solution.py:414
  237.6 132.7 %reduce-scatter.5.cloned.1.call-start = ((), (), s32[]{:S(2)}) async-start(), calls=%async_computation.15 | async-start | bytes 3829760 | tf_op jit(solution)/shard_map/reduce_scatter | solution.py:438
  238.5 5.2 %collective-permute-start.21 = (bf16[48,1280]{1,0:T(8,128)(2,1)S(1)}, bf16[48,1280]{1,0:T(8,128)(2,1)S(1)}, u32[]{:S(2)}, u32[]{:S(2)}) collective-permute-start(bf16[48,1280]{1,0:T(8,128)(2,1)S(1)} %copy-done.23), channel_id=1, source_target_pairs={{12,11},{13,8},{14,9},{15,10},{28,27},{29,24},{30,25},{31,26},{44,... | collective-permute-start | bytes 368648 | tf_op jit(solution)/shard_map/ppermute | solution.py:36
  239.8 3.9 %collective-permute-start.20 = (bf16[48,1280]{1,0:T(8,128)(2,1)S(1)}, bf16[48,1280]{1,0:T(8,128)(2,1)S(1)}, u32[]{:S(2)}, u32[]{:S(2)}) collective-permute-start(bf16[48,1280]{1,0:T(8,128)(2,1)S(1)} %copy-done.23), channel_id=1, source_target_pairs={{12,10},{13,11},{14,8},{15,9},{28,26},{29,27},{30,24},{31,25},{44,... | collective-permute-start | bytes 368648 | tf_op jit(solution)/shard_map/ppermute | solution.py:36
  241.1 3.7 collective-permute-start.19
  242.4 3.7 collective-permute-start.18
  263.1 2.9 collective-permute-start.25
  263.8 2.3 collective-permute-start.24
  264.4 1.6 collective-permute-start.23
  280.3 2.7 collective-permute-start.29
  281.0 2.0 collective-permute-start.28
  281.6 1.4 collective-permute-start.27
  311.2 16.8 %all-to-all-start.10 = ((bf16[16,48,512]{2,1,0:T(8,128)(2,1)}), bf16[16,48,512]{2,1,0:T(8,128)(2,1)S(1)}, u32[]{:S(2)}, u32[]{:S(2)}) async-start(bf16[16,48,512]{2,1,0:T(8,128)(2,1)} %fusion.9), calls=%async_computation.11 | async-start | bytes 1572864 | tf_op jit(solution)/shard_map/all_to_all | solution.py:449
  (28 other events, 361.2 us)
Sparse Core Ops, SparseCore 0:
  10.4 44.4 all-gather.1
  237.8 68.8 reduce-scatter.2
  309.4 60.8 reduce-scatter.4

commit v2 on v1

--- a/solution.py
+++ b/solution.py
@@ -383,7 +383,11 @@
 
     total = jnp.sum(exchange(terms).astype(f32), axis=0)
     leaving = total.astype(bf16)
+    leaving, merged, normed = lax.optimization_barrier((leaving, merged, normed))
     arrived = [permute(leaving, across(s, SECTIONS - 1)) for s in range(SECTIONS - 1)]
+    merger_grad = merger_grads(merged, grad_before, activated, visual_grad_full)
+    *arrived, merger_grad = lax.optimization_barrier((*arrived, merger_grad))
+    merger_grad = lax.psum_scatter(merger_grad, "dp", scatter_dimension=0, tiled=False)
     for term in arrived:
         total = total + term.astype(f32)
     grad_own = unit_back(own.astype(f32), total)
@@ -405,15 +409,7 @@
         total = jnp.sum(exchange(terms).astype(f32), axis=0)
         grad_own = grad_own.astype(f32) + unit_back(saved[0].astype(f32), total)
         grad_own = grad_own.astype(bf16)
-        if layer == SECTIONS - 1:
-            merged, grad_own = lax.optimization_barrier((merged, grad_own))
-            merger_grad = merger_grads(merged, grad_before, activated, visual_grad_full)
         grads = to_section(grad_own, layer, layer - 1)
-        if layer == SECTIONS - 1:
-            place_ref, merger_grad = lax.optimization_barrier((place_ref, merger_grad))
-            merger_grad = lax.psum_scatter(
-                merger_grad, "dp", scatter_dimension=0, tiled=False
-            )
         grad_own = grads[0]
     (joint_grad,) = call(
         last_kernel,

time: 382 us -> 371 us (0.971)
  waiting for transfers between devices: 128 us -> 107 us
  starting transfers between devices: 44.8 us -> 63.9 us
  blocking collectives: 109 us -> 102 us
    reduce_scatter x1, waiting for transfers between devices: 17.9 us -> 0.01 us  [local(): lax.psum_scatter(merger_grad, 'dp', scatter_dimension=0, tiled=False)]
    all_to_all x1, starting transfers between devices: 7.02 us -> 17 us  [local(): visual = lax.all_to_all(visual_terms, ('section', 'mp'), 0, 0)]
    all_to_all x2 -> x3, waiting for transfers between devices: 11.9 us -> 20.2 us  [exchange(): return lax.all_to_all(value, 'mp', 0, 0)]
    ppermute x30, waiting for transfers between devices: 37.4 us -> 30 us  [permute(): return lax.ppermute(value, ('section', 'mp'), pairs)]
    all_to_all x8 -> x7, blocking collectives: 84.3 us -> 77.4 us  [exchange(): return lax.all_to_all(value, 'mp', 0, 0)]
    ppermute x30, starting transfers between devices: 29.3 us -> 34.9 us  [permute(): return lax.ppermute(value, ('section', 'mp'), pairs)]
    all_to_all x2 -> x3, starting transfers between devices: 8.4 us -> 11.9 us  [exchange(): return lax.all_to_all(value, 'mp', 0, 0)]
    unnamed x48 -> x44, local copies, waits for them, and re-layouts: 18.3 us -> 15.8 us
  transfers between devices with their start and end apart: 36 -> 37, of which waited for: 17 -> 14; matrix products, arithmetic and copies ran while one was open for 5% -> 6% of each run, Pallas kernels for 3% -> 6%
where the time goes in v2:
time: 371 us; the launch traced here: 369 us
  waiting for transfers between devices  107 us (29%)
  blocking collectives  102 us (27%)
  starting transfers between devices  63.9 us (17%)
  Pallas kernels  35.5 us (10%)
  local copies, waits for them, and re-layouts  22 us (6%)
  between operations  14.6 us (4%)
  other arithmetic  13.9 us (4%)
  matrix products  10.7 us (3%)
    all_to_all x7, blocking collectives, exchange(): return lax.all_to_all(value, 'mp', 0, 0)  77.4 us
    reduce_scatter x1, waiting for transfers between devices, local(): lax.psum_scatter(joint_grad, 'dp', scatter_dimension=0, tiled=True)  37.7 us
    ppermute x30, starting transfers between devices, permute(): return lax.ppermute(value, ('section', 'mp'), pairs)  34.9 us
    ppermute x30, waiting for transfers between devices, permute(): return lax.ppermute(value, ('section', 'mp'), pairs)  30 us
    pallas_call x10, Pallas kernels, call(): pl.pallas_call(kernel, in_specs=[pl.BlockSpec(memory_space=pltpu.SMEM)] +...  29.9 us
    all_gather x1, blocking collectives, local(): visual_grad_full = lax.all_gather(visual_grad, ('section', 'mp'), axis=0)  24.2 us
    all_to_all x3, waiting for transfers between devices, exchange(): return lax.all_to_all(value, 'mp', 0, 0)  20.2 us
    all_to_all x1, starting transfers between devices, local(): visual = lax.all_to_all(visual_terms, ('section', 'mp'), 0, 0)  17 us
  transfers between devices with their start and end apart: 37, of which 14 were waited for; matrix products, arithmetic and copies ran while one was open for 6% of the time, Pallas kernels for 6%

profile of v2, /device:TPU:6, one launch (start us, length us, event | category | flops | bytes accessed | tf_op | source)
XLA Modules:
  0.0 369.1 jit_solution(14166513708009479048)
XLA Ops:
  14.4 24.2 %all_gather.6.visual_grad = bf16[16,48,512]{2,1,0:T(8,128)(2,1)S(1)} all-gather(bf16[1,48,512]{2,1,0:T(8,128)(2,1)S(1)} %bitcast.117), channel_id=1, replica_groups=mesh['dp'=16,'section'=4,'mp'=4] {'section','mp'}, dimensions={0}, use_global_device_ids=true | all-gather | bytes 835584 | tf_op jit(solution)/shard_map/all_gather | solution.py:320
  38.7 4.8 %fusion.13.grad_act = f32[48,320]{1,0:T(8,128)} fusion(bf16[16,48,512]{2,1,0:T(8,128)(2,1)S(1)} %all_gather.6.visual_grad, bf16[40,16,8,512]{3,2,1,0:T(8,128)(2,1)} %bitcast.109), kind=kOutput, calls=%fused_computation.10 | convolution fusion | flops 251658240 | bytes 6090752 | tf_op jit(solution)/shard_map/jtf,rjf->tr/dot_general | solution.py:321
  43.5 11.4 %all-gather.2.cloned.1.call-done.weight = bf16[1280,1344]{1,0:T(8,128)(2,1)} async-done(((bf16[80,1344]{1,0:T(8,128)(2,1)}), bf16[1280,1344]{1,0:T(8,128)(2,1)}) %all-gather.2.cloned.1.call-update) | async-done | bytes 3440656 | tf_op jit(solution)/shard_map/all_gather | solution.py:297
  56.9 3.1 shard_map.137
  60.1 4.3 %all-to-all-start = ((bf16[4,48,1280]{2,1,0:T(8,128)(2,1)}), bf16[4,48,1280]{2,1,0:T(8,128)(2,1)S(1)}, u32[]{:S(2)}, u32[]{:S(2)}) async-start(bf16[4,48,1280]{2,1,0:T(8,128)(2,1)} %shard_map.137), calls=%async_computation | async-start | bytes 983040 | tf_op jit(solution)/shard_map/all_to_all | solution.py:51
  64.4 9.5 %all-to-all-done = bf16[4,48,1280]{2,1,0:T(8,128)(2,1)S(1)} async-done(((bf16[4,48,1280]{2,1,0:T(8,128)(2,1)}), bf16[4,48,1280]{2,1,0:T(8,128)(2,1)S(1)}, u32[]{:S(2)}, u32[]{:S(2)}) %all-to-all-start) | async-done | bytes 491552 | tf_op jit(solution)/shard_map/all_to_all | solution.py:51
  81.2 11.1 %all_to_all.55 = bf16[4,48,1280]{2,1,0:T(8,128)(2,1)S(1)} all-to-all(bf16[4,48,1280]{2,1,0:T(8,128)(2,1)S(1)} %shard_map.138), channel_id=1, replica_groups=mesh['dp'=16,'section'=4,'mp'=4] {'mp'}, dimensions={0} | all-to-all | bytes 983040 | tf_op jit(solution)/shard_map/all_to_all | solution.py:51
  95.1 2.4 shard_map.139
  97.6 10.3 %all_to_all.56 = bf16[4,48,1280]{2,1,0:T(8,128)(2,1)S(1)} all-to-all(bf16[4,48,1280]{2,1,0:T(8,128)(2,1)S(1)} %shard_map.139), channel_id=1, replica_groups=mesh['dp'=16,'section'=4,'mp'=4] {'mp'}, dimensions={0} | all-to-all | bytes 983040 | tf_op jit(solution)/shard_map/all_to_all | solution.py:51
  113.2 21.6 %collective-permute-done.11.x3 = bf16[48,1280]{1,0:T(8,128)(2,1)S(1)} collective-permute-done((bf16[48,1280]{1,0:T(8,128)(2,1)S(1)}, bf16[48,1280]{1,0:T(8,128)(2,1)S(1)}, u32[]{:S(2)}, u32[]{:S(2)}) %collective-permute-start.11) | collective-permute-done | bytes 122912 | tf_op jit(solution)/shard_map/ppermute | solution.py:36
  138.4 2.4 shard_map.140
  140.8 10.6 %all_to_all.57 = bf16[4,48,1280]{2,1,0:T(8,128)(2,1)S(1)} all-to-all(bf16[4,48,1280]{2,1,0:T(8,128)(2,1)S(1)} %shard_map.140), channel_id=1, replica_groups=mesh['dp'=16,'section'=4,'mp'=4] {'mp'}, dimensions={0} | all-to-all | bytes 983040 | tf_op jit(solution)/shard_map/all_to_all | solution.py:51
  158.8 3.5 all-to-all-start.4
  162.3 7.8 %all-to-all-done.4.blocks = bf16[4,48,1280]{2,1,0:T(8,128)(2,1)S(1)} async-done(((bf16[4,48,1280]{2,1,0:T(8,128)(2,1)}), bf16[4,48,1280]{2,1,0:T(8,128)(2,1)S(1)}, u32[]{:S(2)}, u32[]{:S(2)}) %all-to-all-start.4) | async-done | bytes 491552 | tf_op jit(solution)/shard_map/all_to_all | solution.py:51
  173.0 3.4 shard_map.141
  176.9 4.1 %all-to-all-start.5 = ((bf16[4,48,1280]{2,1,0:T(8,128)(2,1)}), bf16[4,48,1280]{2,1,0:T(8,128)(2,1)}, u32[]{:S(2)}, u32[]{:S(2)}) async-start(bf16[4,48,1280]{2,1,0:T(8,128)(2,1)} %get-tuple-element.37), calls=%async_computation.5 | async-start | bytes 983040 | tf_op jit(solution)/shard_map/all_to_all | solution.py:51
  186.2 2.9 all-to-all-done.5
  194.8 5.5 %shard_map.143 = bf16[16,320,832]{2,1,0:T(8,128)(2,1)S(1)} custom-call(bf16[16,48,320]{2,1,0:T(8,128)(2,1)S(1)} %get-tuple-element.41.merged, bf16[48,320]{1,0:T(8,128)(2,1)S(1)} %copy-done.14, bf16[48,320]{1,0:T(8,128)(2,1)S(1)} %get-tuple-element.61.activated, bf16[16,48,512]{2,1,0:T(8,128)(2,1)S(1)} %all_gather.6.visual_grad), custom_call_target="tpu_custom_call" | custom-call | flops 408944640 | bytes 17039360 | tf_op jit(solution)/shard_map/pallas_call | solution.py:241
  200.3 3.5 copy-done.5
  207.3 10.3 %all_to_all.58 = bf16[4,48,1280]{2,1,0:T(8,128)(2,1)S(1)} all-to-all(bf16[4,48,1280]{2,1,0:T(8,128)(2,1)S(1)} %broadcast_in_dim.136), channel_id=1, replica_groups=mesh['dp'=16,'section'=4,'mp'=4] {'mp'}, dimensions={0} | all-to-all | bytes 983040 | tf_op jit(solution)/shard_map/all_to_all | solution.py:51
  217.8 3.5 shard_map.144
  221.3 10.3 %all_to_all.59 = bf16[4,48,1280]{2,1,0:T(8,128)(2,1)S(1)} all-to-all(bf16[4,48,1280]{2,1,0:T(8,128)(2,1)S(1)} %get-tuple-element.48), channel_id=1, replica_groups=mesh['dp'=16,'section'=4,'mp'=4] {'mp'}, dimensions={0} | all-to-all | bytes 983040 | tf_op jit(solution)/shard_map/all_to_all | solution.py:51
  232.0 6.7 %collective-permute-start.21 = (bf16[48,1280]{1,0:T(8,128)(2,1)S(1)}, bf16[48,1280]{1,0:T(8,128)(2,1)S(1)}, u32[]{:S(2)}, u32[]{:S(2)}) collective-permute-start(bf16[48,1280]{1,0:T(8,128)(2,1)S(1)} %fusion.25), channel_id=1, source_target_pairs={{12,11},{13,8},{14,9},{15,10},{28,27},{29,24},{30,25},{31,26},{44,... | collective-permute-start | bytes 368648 | tf_op jit(solution)/shard_map/ppermute | solution.py:36
  245.3 3.6 shard_map.145
  248.9 14.5 %all_to_all.60 = bf16[4,48,1280]{2,1,0:T(8,128)(2,1)S(1)} all-to-all(bf16[4,48,1280]{2,1,0:T(8,128)(2,1)S(1)} %get-tuple-element.51), channel_id=1, replica_groups=mesh['dp'=16,'section'=4,'mp'=4] {'mp'}, dimensions={0} | all-to-all | bytes 983040 | tf_op jit(solution)/shard_map/all_to_all | solution.py:51
  266.7 3.6 shard_map.146
  270.3 10.3 %all_to_all.61 = bf16[4,48,1280]{2,1,0:T(8,128)(2,1)S(1)} all-to-all(bf16[4,48,1280]{2,1,0:T(8,128)(2,1)S(1)} %get-tuple-element.54), channel_id=1, replica_groups=mesh['dp'=16,'section'=4,'mp'=4] {'mp'}, dimensions={0} | all-to-all | bytes 983040 | tf_op jit(solution)/shard_map/all_to_all | solution.py:51
  283.7 3.9 %shard_map.147 = bf16[1280,1344]{1,0:T(8,128)(2,1)S(1)} custom-call(s32[1]{0:T(128)} %bitcast.12.place_ref._, s32[192,1]{1,0:T(8,128)S(1)} %broadcast_in_dim_tile.8.down, s32[1,192]{1,0:T(1,128)S(1)} %broadcast_in_dim_tile.7.across_ref, bf16[48,1280]{1,0:T(8,128)(2,1)S(1)} %collective-permute-done.26.g0, bf16[48,1280]{1,0:T(8,128)(2,1)S(1)} %collective-permute-done.27.g1, ...), custom_call_target="tpu_custom_call" | custom-call | flops 1321205760 | bytes 10813440 | tf_op jit(solution)/shard_map/pallas_call | solution.py:262
  289.5 4.5 %fusion.9 = bf16[16,48,512]{2,1,0:T(8,128)(2,1)} fusion(bf16[40,16,8,512]{3,2,1,0:T(8,128)(2,1)} %bitcast.110, bf16[48,320]{1,0:T(8,128)(2,1)S(1)} %get-tuple-element.61.activated), kind=kOutput, calls=%fused_computation.7 | convolution fusion | flops 252051456 | bytes 6060032 | tf_op jit(solution)/shard_map/tr,rjf->jtf/dot_general | solution.py:439
  294.0 17.0 %all-to-all-start.10 = ((bf16[16,48,512]{2,1,0:T(8,128)(2,1)}), bf16[16,48,512]{2,1,0:T(8,128)(2,1)S(1)}, u32[]{:S(2)}, u32[]{:S(2)}) async-start(bf16[16,48,512]{2,1,0:T(8,128)(2,1)} %fusion.9), calls=%async_computation.11 | async-start | bytes 1572864 | tf_op jit(solution)/shard_map/all_to_all | solution.py:445
  312.9 7.6 %all-to-all-done.10 = bf16[16,48,512]{2,1,0:T(8,128)(2,1)S(1)} async-done(((bf16[16,48,512]{2,1,0:T(8,128)(2,1)}), bf16[16,48,512]{2,1,0:T(8,128)(2,1)S(1)}, u32[]{:S(2)}, u32[]{:S(2)}) %all-to-all-start.10) | async-done | bytes 786464 | tf_op jit(solution)/shard_map/all_to_all | solution.py:445
  321.8 37.7 %reduce-scatter.5.cloned.1.call-done = bf16[80,1344]{1,0:T(8,128)(2,1)} async-done(((bf16[1280,1344]{1,0:T(8,128)(2,1)}), bf16[80,1344]{1,0:T(8,128)(2,1)}) %reduce-scatter.5.cloned.1.call-update) | async-done | bytes 215056 | tf_op jit(solution)/shard_map/reduce_scatter | solution.py:434
  (173 shorter events, 74.5 us)
Async XLA Ops:
  7.2 47.7 %all-gather.2.cloned.1.call-start = ((), (), s32[]{:S(2)}) async-start(), calls=%async_computation.13 | async-start | bytes 3829760 | tf_op jit(solution)/shard_map/all_gather | solution.py:297
  60.1 13.8 %all-to-all-start = ((bf16[4,48,1280]{2,1,0:T(8,128)(2,1)}), bf16[4,48,1280]{2,1,0:T(8,128)(2,1)S(1)}, u32[]{:S(2)}, u32[]{:S(2)}) async-start(bf16[4,48,1280]{2,1,0:T(8,128)(2,1)} %shard_map.137), calls=%async_computation | async-start | bytes 983040 | tf_op jit(solution)/shard_map/all_to_all | solution.py:51
  74.0 2.7 collective-permute-start.3
  74.7 2.0 collective-permute-start.2
  92.4 2.7 collective-permute-start.7
  93.1 2.0 collective-permute-start.6
  93.7 1.4 collective-permute-start.5
  108.0 26.8 %collective-permute-start.11 = (bf16[48,1280]{1,0:T(8,128)(2,1)S(1)}, bf16[48,1280]{1,0:T(8,128)(2,1)S(1)}, u32[]{:S(2)}, u32[]{:S(2)}) collective-permute-start(bf16[48,1280]{1,0:T(8,128)(2,1)S(1)} %add_convert_fusion.1), channel_id=1, source_target_pairs={{8,15},{9,12},{10,13},{11,14},{24,31},{25,28},{26,29},{27,30},{40,... | collective-permute-start | bytes 368648 | tf_op jit(solution)/shard_map/ppermute | solution.py:36
  109.3 26.9 %collective-permute-start.10 = (bf16[48,1280]{1,0:T(8,128)(2,1)S(1)}, bf16[48,1280]{1,0:T(8,128)(2,1)S(1)}, u32[]{:S(2)}, u32[]{:S(2)}) collective-permute-start(bf16[48,1280]{1,0:T(8,128)(2,1)S(1)} %add_convert_fusion.1), channel_id=1, source_target_pairs={{8,14},{9,15},{10,12},{11,13},{24,30},{25,31},{26,28},{27,29},{40,... | collective-permute-start | bytes 368648 | tf_op jit(solution)/shard_map/ppermute | solution.py:36
  110.6 27.2 %collective-permute-start.9 = (bf16[48,1280]{1,0:T(8,128)(2,1)S(1)}, bf16[48,1280]{1,0:T(8,128)(2,1)S(1)}, u32[]{:S(2)}, u32[]{:S(2)}) collective-permute-start(bf16[48,1280]{1,0:T(8,128)(2,1)S(1)} %add_convert_fusion.1), channel_id=1, source_target_pairs={{8,13},{9,14},{10,15},{11,12},{24,29},{25,30},{26,31},{27,28},{40,... | collective-permute-start | bytes 368648 | tf_op jit(solution)/shard_map/ppermute | solution.py:36
  111.9 26.5 %collective-permute-start.8 = (bf16[48,1280]{1,0:T(8,128)(2,1)S(1)}, bf16[48,1280]{1,0:T(8,128)(2,1)S(1)}, u32[]{:S(2)}, u32[]{:S(2)}) collective-permute-start(bf16[48,1280]{1,0:T(8,128)(2,1)S(1)} %add_convert_fusion.1), channel_id=1, source_target_pairs={{8,12},{9,13},{10,14},{11,15},{24,28},{25,29},{26,30},{27,31},{40,... | collective-permute-start | bytes 368648 | tf_op jit(solution)/shard_map/ppermute | solution.py:36
  151.6 4.1 %collective-permute-start.14 = (bf16[48,1280]{1,0:T(8,128)(2,1)S(1)}, bf16[48,1280]{1,0:T(8,128)(2,1)S(1)}, u32[]{:S(2)}, u32[]{:S(2)}) collective-permute-start(bf16[48,1280]{1,0:T(8,128)(2,1)S(1)} %add_convert_fusion), channel_id=1, source_target_pairs={{12,8},{13,9},{14,10},{15,11},{28,24},{29,25},{30,26},{31,27},{44,... | collective-permute-start | bytes 368648 | tf_op jit(solution)/shard_map/ppermute | solution.py:36
  152.9 3.7 %collective-permute-start.13 = (bf16[48,1280]{1,0:T(8,128)(2,1)S(1)}, bf16[48,1280]{1,0:T(8,128)(2,1)S(1)}, u32[]{:S(2)}, u32[]{:S(2)}) collective-permute-start(bf16[48,1280]{1,0:T(8,128)(2,1)S(1)} %add_convert_fusion), channel_id=1, source_target_pairs={{12,4},{13,5},{14,6},{15,7},{28,20},{29,21},{30,22},{31,23},{44,36... | collective-permute-start | bytes 368648 | tf_op jit(solution)/shard_map/ppermute | solution.py:36
  154.2 3.7 %collective-permute-start.12 = (bf16[48,1280]{1,0:T(8,128)(2,1)S(1)}, bf16[48,1280]{1,0:T(8,128)(2,1)S(1)}, u32[]{:S(2)}, u32[]{:S(2)}) collective-permute-start(bf16[48,1280]{1,0:T(8,128)(2,1)S(1)} %add_convert_fusion), channel_id=1, source_target_pairs={{12,0},{13,1},{14,2},{15,3},{28,16},{29,17},{30,18},{31,19},{44,32... | collective-permute-start | bytes 368648 | tf_op jit(solution)/shard_map/ppermute | solution.py:36
  158.8 11.3 %all-to-all-start.4 = ((bf16[4,48,1280]{2,1,0:T(8,128)(2,1)}), bf16[4,48,1280]{2,1,0:T(8,128)(2,1)S(1)}, u32[]{:S(2)}, u32[]{:S(2)}) async-start(bf16[4,48,1280]{2,1,0:T(8,128)(2,1)} %broadcast_in_dim.134), calls=%async_computation.4 | async-start | bytes 983040 | tf_op jit(solution)/shard_map/all_to_all | solution.py:51
  176.9 12.1 %all-to-all-start.5 = ((bf16[4,48,1280]{2,1,0:T(8,128)(2,1)}), bf16[4,48,1280]{2,1,0:T(8,128)(2,1)}, u32[]{:S(2)}, u32[]{:S(2)}) async-start(bf16[4,48,1280]{2,1,0:T(8,128)(2,1)} %get-tuple-element.37), calls=%async_computation.5 | async-start | bytes 983040 | tf_op jit(solution)/shard_map/all_to_all | solution.py:51
  181.1 108.4 %reduce-scatter.3.cloned.1.call-start = ((), (), s32[]{:S(2)}) async-start(), calls=%async_computation.14 | async-start | bytes 9748480 | tf_op jit(solution)/shard_map/reduce_scatter | solution.py:390
  190.9 13.0 %collective-permute-start.17 = (bf16[48,1280]{1,0:T(8,128)(2,1)}, bf16[48,1280]{1,0:T(8,128)(2,1)S(1)}, u32[]{:S(2)}, u32[]{:S(2)}) collective-permute-start(bf16[48,1280]{1,0:T(8,128)(2,1)} %convert_element_type.142), channel_id=1, source_target_pairs={{8,12},{9,13},{10,14},{11,15},{24,28},{25,29},{26,30},{27,31},{40,... | collective-permute-start | bytes 368648 | tf_op jit(solution)/shard_map/ppermute | solution.py:36
  192.2 11.7 %collective-permute-start.16 = (bf16[48,1280]{1,0:T(8,128)(2,1)}, bf16[48,1280]{1,0:T(8,128)(2,1)}, u32[]{:S(2)}, u32[]{:S(2)}) collective-permute-start(bf16[48,1280]{1,0:T(8,128)(2,1)} %convert_element_type.142), channel_id=1, source_target_pairs={{4,12},{5,13},{6,14},{7,15},{20,28},{21,29},{22,30},{23,31},{36,44... | collective-permute-start | bytes 368648 | tf_op jit(solution)/shard_map/ppermute | solution.py:36
  193.5 10.4 %collective-permute-start.15 = (bf16[48,1280]{1,0:T(8,128)(2,1)}, bf16[48,1280]{1,0:T(8,128)(2,1)}, u32[]{:S(2)}, u32[]{:S(2)}) collective-permute-start(bf16[48,1280]{1,0:T(8,128)(2,1)} %convert_element_type.142), channel_id=1, source_target_pairs={{0,12},{1,13},{2,14},{3,15},{16,28},{17,29},{18,30},{19,31},{32,44... | collective-permute-start | bytes 368648 | tf_op jit(solution)/shard_map/ppermute | solution.py:36
  203.9 155.6 %reduce-scatter.5.cloned.1.call-start = ((), (), s32[]{:S(2)}) async-start(), calls=%async_computation.15 | async-start | bytes 3829760 | tf_op jit(solution)/shard_map/reduce_scatter | solution.py:434
  232.0 10.9 %collective-permute-start.21 = (bf16[48,1280]{1,0:T(8,128)(2,1)S(1)}, bf16[48,1280]{1,0:T(8,128)(2,1)S(1)}, u32[]{:S(2)}, u32[]{:S(2)}) collective-permute-start(bf16[48,1280]{1,0:T(8,128)(2,1)S(1)} %fusion.25), channel_id=1, source_target_pairs={{12,11},{13,8},{14,9},{15,10},{28,27},{29,24},{30,25},{31,26},{44,... | collective-permute-start | bytes 368648 | tf_op jit(solution)/shard_map/ppermute | solution.py:36
  238.7 4.2 %collective-permute-start.20 = (bf16[48,1280]{1,0:T(8,128)(2,1)S(1)}, bf16[48,1280]{1,0:T(8,128)(2,1)S(1)}, u32[]{:S(2)}, u32[]{:S(2)}) collective-permute-start(bf16[48,1280]{1,0:T(8,128)(2,1)S(1)} %fusion.25), channel_id=1, source_target_pairs={{12,10},{13,11},{14,8},{15,9},{28,26},{29,27},{30,24},{31,25},{44,... | collective-permute-start | bytes 368648 | tf_op jit(solution)/shard_map/ppermute | solution.py:36
  240.3 3.7 %collective-permute-start.19 = (bf16[48,1280]{1,0:T(8,128)(2,1)S(1)}, bf16[48,1280]{1,0:T(8,128)(2,1)S(1)}, u32[]{:S(2)}, u32[]{:S(2)}) collective-permute-start(bf16[48,1280]{1,0:T(8,128)(2,1)S(1)} %fusion.25), channel_id=1, source_target_pairs={{12,9},{13,10},{14,11},{15,8},{28,25},{29,26},{30,27},{31,24},{44,... | collective-permute-start | bytes 368648 | tf_op jit(solution)/shard_map/ppermute | solution.py:36
  241.6 3.7 %collective-permute-start.18 = (bf16[48,1280]{1,0:T(8,128)(2,1)S(1)}, bf16[48,1280]{1,0:T(8,128)(2,1)S(1)}, u32[]{:S(2)}, u32[]{:S(2)}) collective-permute-start(bf16[48,1280]{1,0:T(8,128)(2,1)S(1)} %fusion.25), channel_id=1, source_target_pairs={{12,8},{13,9},{14,10},{15,11},{28,24},{29,25},{30,26},{31,27},{44,... | collective-permute-start | bytes 368648 | tf_op jit(solution)/shard_map/ppermute | solution.py:36
  263.7 2.9 collective-permute-start.25
  264.4 2.3 collective-permute-start.24
  265.1 1.6 collective-permute-start.23
  280.9 2.7 collective-permute-start.29
  281.6 2.0 collective-permute-start.28
  282.3 1.4 collective-permute-start.27
  294.0 26.4 %all-to-all-start.10 = ((bf16[16,48,512]{2,1,0:T(8,128)(2,1)}), bf16[16,48,512]{2,1,0:T(8,128)(2,1)S(1)}, u32[]{:S(2)}, u32[]{:S(2)}) async-start(bf16[16,48,512]{2,1,0:T(8,128)(2,1)} %fusion.9), calls=%async_computation.11 | async-start | bytes 1572864 | tf_op jit(solution)/shard_map/all_to_all | solution.py:445
  (27 other events, 280.0 us)
Sparse Core Ops, SparseCore 0:
  10.4 44.4 all-gather.1
  204.0 71.0 reduce-scatter.2
  289.6 69.8 reduce-scatter.4

commit v3 on v2

--- a/solution.py
+++ b/solution.py
@@ -388,6 +388,7 @@
     merger_grad = merger_grads(merged, grad_before, activated, visual_grad_full)
     *arrived, merger_grad = lax.optimization_barrier((*arrived, merger_grad))
     merger_grad = lax.psum_scatter(merger_grad, "dp", scatter_dimension=0, tiled=False)
+    total = leaving.astype(f32)
     for term in arrived:
         total = total + term.astype(f32)
     grad_own = unit_back(own.astype(f32), total)

time: 371 us -> 371 us (level)
    unnamed x44 -> x40, local copies, waits for them, and re-layouts: 15.8 us -> 16.4 us
where the time goes in v3:
time: 371 us; the launch traced here: 370 us
  waiting for transfers between devices  107 us (29%)
  blocking collectives  102 us (27%)
  starting transfers between devices  64.6 us (17%)
  Pallas kernels  35.4 us (10%)
  local copies, waits for them, and re-layouts  22.7 us (6%)
  between operations  14.6 us (4%)
  other arithmetic  13.2 us (4%)
  matrix products  10.8 us (3%)
    all_to_all x7, blocking collectives, exchange(): return lax.all_to_all(value, 'mp', 0, 0)  77.4 us
    reduce_scatter x1, waiting for transfers between devices, local(): lax.psum_scatter(joint_grad, 'dp', scatter_dimension=0, tiled=True)  37.7 us
    ppermute x30, starting transfers between devices, permute(): return lax.ppermute(value, ('section', 'mp'), pairs)  35.6 us
    ppermute x30, waiting for transfers between devices, permute(): return lax.ppermute(value, ('section', 'mp'), pairs)  30 us
    pallas_call x10, Pallas kernels, call(): pl.pallas_call(kernel, in_specs=[pl.BlockSpec(memory_space=pltpu.SMEM)] +...  29.9 us
    all_gather x1, blocking collectives, local(): visual_grad_full = lax.all_gather(visual_grad, ('section', 'mp'), axis=0)  24.2 us
    all_to_all x3, waiting for transfers between devices, exchange(): return lax.all_to_all(value, 'mp', 0, 0)  20.2 us
    all_to_all x1, starting transfers between devices, local(): visual = lax.all_to_all(visual_terms, ('section', 'mp'), 0, 0)  17.1 us
  transfers between devices with their start and end apart: 37, of which 14 were waited for; matrix products, arithmetic and copies ran while one was open for 6% of the time, Pallas kernels for 6%

profile of v3, /device:TPU:6, one launch (start us, length us, event | category | flops | bytes accessed | tf_op | source)
XLA Modules:
  0.0 369.9 jit_solution(10925649772457469671)
XLA Ops:
  14.4 24.2 %all_gather.6.visual_grad = bf16[16,48,512]{2,1,0:T(8,128)(2,1)S(1)} all-gather(bf16[1,48,512]{2,1,0:T(8,128)(2,1)S(1)} %bitcast.117), channel_id=1, replica_groups=mesh['dp'=16,'section'=4,'mp'=4] {'section','mp'}, dimensions={0}, use_global_device_ids=true | all-gather | bytes 835584 | tf_op jit(solution)/shard_map/all_gather | solution.py:320
  38.7 4.8 %fusion.13.grad_act = f32[48,320]{1,0:T(8,128)} fusion(bf16[16,48,512]{2,1,0:T(8,128)(2,1)S(1)} %all_gather.6.visual_grad, bf16[40,16,8,512]{3,2,1,0:T(8,128)(2,1)} %bitcast.109), kind=kOutput, calls=%fused_computation.10 | convolution fusion | flops 251658240 | bytes 6090752 | tf_op jit(solution)/shard_map/jtf,rjf->tr/dot_general | solution.py:321
  43.5 11.4 %all-gather.2.cloned.1.call-done.weight = bf16[1280,1344]{1,0:T(8,128)(2,1)} async-done(((bf16[80,1344]{1,0:T(8,128)(2,1)}), bf16[1280,1344]{1,0:T(8,128)(2,1)}) %all-gather.2.cloned.1.call-update) | async-done | bytes 3440656 | tf_op jit(solution)/shard_map/all_gather | solution.py:297
  56.9 3.1 shard_map.137
  60.1 4.3 %all-to-all-start = ((bf16[4,48,1280]{2,1,0:T(8,128)(2,1)}), bf16[4,48,1280]{2,1,0:T(8,128)(2,1)S(1)}, u32[]{:S(2)}, u32[]{:S(2)}) async-start(bf16[4,48,1280]{2,1,0:T(8,128)(2,1)} %shard_map.137), calls=%async_computation | async-start | bytes 983040 | tf_op jit(solution)/shard_map/all_to_all | solution.py:51
  64.4 9.5 %all-to-all-done = bf16[4,48,1280]{2,1,0:T(8,128)(2,1)S(1)} async-done(((bf16[4,48,1280]{2,1,0:T(8,128)(2,1)}), bf16[4,48,1280]{2,1,0:T(8,128)(2,1)S(1)}, u32[]{:S(2)}, u32[]{:S(2)}) %all-to-all-start) | async-done | bytes 491552 | tf_op jit(solution)/shard_map/all_to_all | solution.py:51
  81.2 11.1 %all_to_all.55 = bf16[4,48,1280]{2,1,0:T(8,128)(2,1)S(1)} all-to-all(bf16[4,48,1280]{2,1,0:T(8,128)(2,1)S(1)} %shard_map.138), channel_id=1, replica_groups=mesh['dp'=16,'section'=4,'mp'=4] {'mp'}, dimensions={0} | all-to-all | bytes 983040 | tf_op jit(solution)/shard_map/all_to_all | solution.py:51
  95.1 2.4 shard_map.139
  97.6 10.3 %all_to_all.56 = bf16[4,48,1280]{2,1,0:T(8,128)(2,1)S(1)} all-to-all(bf16[4,48,1280]{2,1,0:T(8,128)(2,1)S(1)} %shard_map.139), channel_id=1, replica_groups=mesh['dp'=16,'section'=4,'mp'=4] {'mp'}, dimensions={0} | all-to-all | bytes 983040 | tf_op jit(solution)/shard_map/all_to_all | solution.py:51
  113.2 21.6 %collective-permute-done.11.x3 = bf16[48,1280]{1,0:T(8,128)(2,1)S(1)} collective-permute-done((bf16[48,1280]{1,0:T(8,128)(2,1)S(1)}, bf16[48,1280]{1,0:T(8,128)(2,1)S(1)}, u32[]{:S(2)}, u32[]{:S(2)}) %collective-permute-start.11) | collective-permute-done | bytes 122912 | tf_op jit(solution)/shard_map/ppermute | solution.py:36
  138.4 2.4 shard_map.140
  140.8 10.6 %all_to_all.57 = bf16[4,48,1280]{2,1,0:T(8,128)(2,1)S(1)} all-to-all(bf16[4,48,1280]{2,1,0:T(8,128)(2,1)S(1)} %shard_map.140), channel_id=1, replica_groups=mesh['dp'=16,'section'=4,'mp'=4] {'mp'}, dimensions={0} | all-to-all | bytes 983040 | tf_op jit(solution)/shard_map/all_to_all | solution.py:51
  158.8 3.5 all-to-all-start.4
  162.3 7.8 %all-to-all-done.4.blocks = bf16[4,48,1280]{2,1,0:T(8,128)(2,1)S(1)} async-done(((bf16[4,48,1280]{2,1,0:T(8,128)(2,1)}), bf16[4,48,1280]{2,1,0:T(8,128)(2,1)S(1)}, u32[]{:S(2)}, u32[]{:S(2)}) %all-to-all-start.4) | async-done | bytes 491552 | tf_op jit(solution)/shard_map/all_to_all | solution.py:51
  172.9 3.4 shard_map.141
  176.9 4.1 %all-to-all-start.5 = ((bf16[4,48,1280]{2,1,0:T(8,128)(2,1)}), bf16[4,48,1280]{2,1,0:T(8,128)(2,1)}, u32[]{:S(2)}, u32[]{:S(2)}) async-start(bf16[4,48,1280]{2,1,0:T(8,128)(2,1)} %get-tuple-element.37), calls=%async_computation.5 | async-start | bytes 983040 | tf_op jit(solution)/shard_map/all_to_all | solution.py:51
  186.2 2.9 all-to-all-done.5
  194.8 5.5 %shard_map.143 = bf16[16,320,832]{2,1,0:T(8,128)(2,1)S(1)} custom-call(bf16[16,48,320]{2,1,0:T(8,128)(2,1)S(1)} %get-tuple-element.41.merged, bf16[48,320]{1,0:T(8,128)(2,1)S(1)} %copy-done.14, bf16[48,320]{1,0:T(8,128)(2,1)S(1)} %get-tuple-element.61.activated, bf16[16,48,512]{2,1,0:T(8,128)(2,1)S(1)} %all_gather.6.visual_grad), custom_call_target="tpu_custom_call" | custom-call | flops 408944640 | bytes 17039360 | tf_op jit(solution)/shard_map/pallas_call | solution.py:241
  200.3 3.5 copy-done.5
  207.3 10.3 %all_to_all.58 = bf16[4,48,1280]{2,1,0:T(8,128)(2,1)S(1)} all-to-all(bf16[4,48,1280]{2,1,0:T(8,128)(2,1)S(1)} %broadcast_in_dim.136), channel_id=1, replica_groups=mesh['dp'=16,'section'=4,'mp'=4] {'mp'}, dimensions={0} | all-to-all | bytes 983040 | tf_op jit(solution)/shard_map/all_to_all | solution.py:51
  217.8 3.5 shard_map.144
  221.3 10.3 %all_to_all.59 = bf16[4,48,1280]{2,1,0:T(8,128)(2,1)S(1)} all-to-all(bf16[4,48,1280]{2,1,0:T(8,128)(2,1)S(1)} %get-tuple-element.48), channel_id=1, replica_groups=mesh['dp'=16,'section'=4,'mp'=4] {'mp'}, dimensions={0} | all-to-all | bytes 983040 | tf_op jit(solution)/shard_map/all_to_all | solution.py:51
  232.0 7.4 %collective-permute-start.21 = (bf16[48,1280]{1,0:T(8,128)(2,1)S(1)}, bf16[48,1280]{1,0:T(8,128)(2,1)S(1)}, u32[]{:S(2)}, u32[]{:S(2)}) collective-permute-start(bf16[48,1280]{1,0:T(8,128)(2,1)S(1)} %fusion.25), channel_id=1, source_target_pairs={{12,11},{13,8},{14,9},{15,10},{28,27},{29,24},{30,25},{31,26},{44,... | collective-permute-start | bytes 368648 | tf_op jit(solution)/shard_map/ppermute | solution.py:36
  246.0 3.6 shard_map.145
  249.6 14.5 %all_to_all.60 = bf16[4,48,1280]{2,1,0:T(8,128)(2,1)S(1)} all-to-all(bf16[4,48,1280]{2,1,0:T(8,128)(2,1)S(1)} %get-tuple-element.51), channel_id=1, replica_groups=mesh['dp'=16,'section'=4,'mp'=4] {'mp'}, dimensions={0} | all-to-all | bytes 983040 | tf_op jit(solution)/shard_map/all_to_all | solution.py:51
  267.4 3.6 shard_map.146
  271.0 10.3 %all_to_all.61 = bf16[4,48,1280]{2,1,0:T(8,128)(2,1)S(1)} all-to-all(bf16[4,48,1280]{2,1,0:T(8,128)(2,1)S(1)} %get-tuple-element.54), channel_id=1, replica_groups=mesh['dp'=16,'section'=4,'mp'=4] {'mp'}, dimensions={0} | all-to-all | bytes 983040 | tf_op jit(solution)/shard_map/all_to_all | solution.py:51
  284.4 3.9 %shard_map.147 = bf16[1280,1344]{1,0:T(8,128)(2,1)S(1)} custom-call(s32[1]{0:T(128)} %bitcast.12.place_ref._, s32[192,1]{1,0:T(8,128)S(1)} %broadcast_in_dim_tile.8.down, s32[1,192]{1,0:T(1,128)S(1)} %broadcast_in_dim_tile.7.across_ref, bf16[48,1280]{1,0:T(8,128)(2,1)S(1)} %collective-permute-done.26.g0, bf16[48,1280]{1,0:T(8,128)(2,1)S(1)} %collective-permute-done.27.g1, ...), custom_call_target="tpu_custom_call" | custom-call | flops 1321205760 | bytes 10813440 | tf_op jit(solution)/shard_map/pallas_call | solution.py:262
  290.1 4.5 %fusion.9 = bf16[16,48,512]{2,1,0:T(8,128)(2,1)} fusion(bf16[40,16,8,512]{3,2,1,0:T(8,128)(2,1)} %bitcast.110, bf16[48,320]{1,0:T(8,128)(2,1)S(1)} %get-tuple-element.61.activated), kind=kOutput, calls=%fused_computation.7 | convolution fusion | flops 252051456 | bytes 6060032 | tf_op jit(solution)/shard_map/tr,rjf->jtf/dot_general | solution.py:440
  294.7 17.1 %all-to-all-start.10 = ((bf16[16,48,512]{2,1,0:T(8,128)(2,1)}), bf16[16,48,512]{2,1,0:T(8,128)(2,1)S(1)}, u32[]{:S(2)}, u32[]{:S(2)}) async-start(bf16[16,48,512]{2,1,0:T(8,128)(2,1)} %fusion.9), calls=%async_computation.11 | async-start | bytes 1572864 | tf_op jit(solution)/shard_map/all_to_all | solution.py:446
  313.6 7.6 %all-to-all-done.10 = bf16[16,48,512]{2,1,0:T(8,128)(2,1)S(1)} async-done(((bf16[16,48,512]{2,1,0:T(8,128)(2,1)}), bf16[16,48,512]{2,1,0:T(8,128)(2,1)S(1)}, u32[]{:S(2)}, u32[]{:S(2)}) %all-to-all-start.10) | async-done | bytes 786464 | tf_op jit(solution)/shard_map/all_to_all | solution.py:446
  322.5 37.7 %reduce-scatter.5.cloned.1.call-done = bf16[80,1344]{1,0:T(8,128)(2,1)} async-done(((bf16[1280,1344]{1,0:T(8,128)(2,1)}), bf16[80,1344]{1,0:T(8,128)(2,1)}) %reduce-scatter.5.cloned.1.call-update) | async-done | bytes 215056 | tf_op jit(solution)/shard_map/reduce_scatter | solution.py:435
  (168 shorter events, 74.5 us)
Async XLA Ops:
  7.2 47.7 %all-gather.2.cloned.1.call-start = ((), (), s32[]{:S(2)}) async-start(), calls=%async_computation.13 | async-start | bytes 3829760 | tf_op jit(solution)/shard_map/all_gather | solution.py:297
  60.1 13.8 %all-to-all-start = ((bf16[4,48,1280]{2,1,0:T(8,128)(2,1)}), bf16[4,48,1280]{2,1,0:T(8,128)(2,1)S(1)}, u32[]{:S(2)}, u32[]{:S(2)}) async-start(bf16[4,48,1280]{2,1,0:T(8,128)(2,1)} %shard_map.137), calls=%async_computation | async-start | bytes 983040 | tf_op jit(solution)/shard_map/all_to_all | solution.py:51
  74.0 2.7 collective-permute-start.3
  74.7 2.0 collective-permute-start.2
  75.4 1.4 collective-permute-start.1
  92.4 2.7 collective-permute-start.7
  93.1 2.0 collective-permute-start.6
  93.7 1.4 collective-permute-start.5
  108.0 26.8 %collective-permute-start.11 = (bf16[48,1280]{1,0:T(8,128)(2,1)S(1)}, bf16[48,1280]{1,0:T(8,128)(2,1)S(1)}, u32[]{:S(2)}, u32[]{:S(2)}) collective-permute-start(bf16[48,1280]{1,0:T(8,128)(2,1)S(1)} %add_convert_fusion.1), channel_id=1, source_target_pairs={{8,15},{9,12},{10,13},{11,14},{24,31},{25,28},{26,29},{27,30},{40,... | collective-permute-start | bytes 368648 | tf_op jit(solution)/shard_map/ppermute | solution.py:36
  109.3 26.9 %collective-permute-start.10 = (bf16[48,1280]{1,0:T(8,128)(2,1)S(1)}, bf16[48,1280]{1,0:T(8,128)(2,1)S(1)}, u32[]{:S(2)}, u32[]{:S(2)}) collective-permute-start(bf16[48,1280]{1,0:T(8,128)(2,1)S(1)} %add_convert_fusion.1), channel_id=1, source_target_pairs={{8,14},{9,15},{10,12},{11,13},{24,30},{25,31},{26,28},{27,29},{40,... | collective-permute-start | bytes 368648 | tf_op jit(solution)/shard_map/ppermute | solution.py:36
  110.6 27.2 %collective-permute-start.9 = (bf16[48,1280]{1,0:T(8,128)(2,1)S(1)}, bf16[48,1280]{1,0:T(8,128)(2,1)S(1)}, u32[]{:S(2)}, u32[]{:S(2)}) collective-permute-start(bf16[48,1280]{1,0:T(8,128)(2,1)S(1)} %add_convert_fusion.1), channel_id=1, source_target_pairs={{8,13},{9,14},{10,15},{11,12},{24,29},{25,30},{26,31},{27,28},{40,... | collective-permute-start | bytes 368648 | tf_op jit(solution)/shard_map/ppermute | solution.py:36
  111.9 26.5 %collective-permute-start.8 = (bf16[48,1280]{1,0:T(8,128)(2,1)S(1)}, bf16[48,1280]{1,0:T(8,128)(2,1)S(1)}, u32[]{:S(2)}, u32[]{:S(2)}) collective-permute-start(bf16[48,1280]{1,0:T(8,128)(2,1)S(1)} %add_convert_fusion.1), channel_id=1, source_target_pairs={{8,12},{9,13},{10,14},{11,15},{24,28},{25,29},{26,30},{27,31},{40,... | collective-permute-start | bytes 368648 | tf_op jit(solution)/shard_map/ppermute | solution.py:36
  151.6 4.1 %collective-permute-start.14 = (bf16[48,1280]{1,0:T(8,128)(2,1)S(1)}, bf16[48,1280]{1,0:T(8,128)(2,1)S(1)}, u32[]{:S(2)}, u32[]{:S(2)}) collective-permute-start(bf16[48,1280]{1,0:T(8,128)(2,1)S(1)} %add_convert_fusion), channel_id=1, source_target_pairs={{12,8},{13,9},{14,10},{15,11},{28,24},{29,25},{30,26},{31,27},{44,... | collective-permute-start | bytes 368648 | tf_op jit(solution)/shard_map/ppermute | solution.py:36
  152.9 3.7 %collective-permute-start.13 = (bf16[48,1280]{1,0:T(8,128)(2,1)S(1)}, bf16[48,1280]{1,0:T(8,128)(2,1)S(1)}, u32[]{:S(2)}, u32[]{:S(2)}) collective-permute-start(bf16[48,1280]{1,0:T(8,128)(2,1)S(1)} %add_convert_fusion), channel_id=1, source_target_pairs={{12,4},{13,5},{14,6},{15,7},{28,20},{29,21},{30,22},{31,23},{44,36... | collective-permute-start | bytes 368648 | tf_op jit(solution)/shard_map/ppermute | solution.py:36
  154.2 3.7 %collective-permute-start.12 = (bf16[48,1280]{1,0:T(8,128)(2,1)S(1)}, bf16[48,1280]{1,0:T(8,128)(2,1)S(1)}, u32[]{:S(2)}, u32[]{:S(2)}) collective-permute-start(bf16[48,1280]{1,0:T(8,128)(2,1)S(1)} %add_convert_fusion), channel_id=1, source_target_pairs={{12,0},{13,1},{14,2},{15,3},{28,16},{29,17},{30,18},{31,19},{44,32... | collective-permute-start | bytes 368648 | tf_op jit(solution)/shard_map/ppermute | solution.py:36
  158.8 11.3 %all-to-all-start.4 = ((bf16[4,48,1280]{2,1,0:T(8,128)(2,1)}), bf16[4,48,1280]{2,1,0:T(8,128)(2,1)S(1)}, u32[]{:S(2)}, u32[]{:S(2)}) async-start(bf16[4,48,1280]{2,1,0:T(8,128)(2,1)} %broadcast_in_dim.134), calls=%async_computation.4 | async-start | bytes 983040 | tf_op jit(solution)/shard_map/all_to_all | solution.py:51
  176.9 12.1 %all-to-all-start.5 = ((bf16[4,48,1280]{2,1,0:T(8,128)(2,1)}), bf16[4,48,1280]{2,1,0:T(8,128)(2,1)}, u32[]{:S(2)}, u32[]{:S(2)}) async-start(bf16[4,48,1280]{2,1,0:T(8,128)(2,1)} %get-tuple-element.37), calls=%async_computation.5 | async-start | bytes 983040 | tf_op jit(solution)/shard_map/all_to_all | solution.py:51
  181.1 109.0 %reduce-scatter.3.cloned.1.call-start = ((), (), s32[]{:S(2)}) async-start(), calls=%async_computation.14 | async-start | bytes 9748480 | tf_op jit(solution)/shard_map/reduce_scatter | solution.py:390
  190.1 13.7 %collective-permute-start.17 = (bf16[48,1280]{1,0:T(8,128)(2,1)S(1)}, bf16[48,1280]{1,0:T(8,128)(2,1)}, u32[]{:S(2)}, u32[]{:S(2)}) collective-permute-start(bf16[48,1280]{1,0:T(8,128)(2,1)S(1)} %reduce_sum.234), channel_id=1, source_target_pairs={{8,12},{9,13},{10,14},{11,15},{24,28},{25,29},{26,30},{27,31},{40,... | collective-permute-start | bytes 368648 | tf_op jit(solution)/shard_map/ppermute | solution.py:36
  191.4 12.4 %collective-permute-start.16 = (bf16[48,1280]{1,0:T(8,128)(2,1)S(1)}, bf16[48,1280]{1,0:T(8,128)(2,1)}, u32[]{:S(2)}, u32[]{:S(2)}) collective-permute-start(bf16[48,1280]{1,0:T(8,128)(2,1)S(1)} %reduce_sum.234), channel_id=1, source_target_pairs={{4,12},{5,13},{6,14},{7,15},{20,28},{21,29},{22,30},{23,31},{36,44... | collective-permute-start | bytes 368648 | tf_op jit(solution)/shard_map/ppermute | solution.py:36
  192.7 11.1 %collective-permute-start.15 = (bf16[48,1280]{1,0:T(8,128)(2,1)S(1)}, bf16[48,1280]{1,0:T(8,128)(2,1)}, u32[]{:S(2)}, u32[]{:S(2)}) collective-permute-start(bf16[48,1280]{1,0:T(8,128)(2,1)S(1)} %reduce_sum.234), channel_id=1, source_target_pairs={{0,12},{1,13},{2,14},{3,15},{16,28},{17,29},{18,30},{19,31},{32,44... | collective-permute-start | bytes 368648 | tf_op jit(solution)/shard_map/ppermute | solution.py:36
  203.9 156.3 %reduce-scatter.5.cloned.1.call-start = ((), (), s32[]{:S(2)}) async-start(), calls=%async_computation.15 | async-start | bytes 3829760 | tf_op jit(solution)/shard_map/reduce_scatter | solution.py:435
  232.0 11.6 %collective-permute-start.21 = (bf16[48,1280]{1,0:T(8,128)(2,1)S(1)}, bf16[48,1280]{1,0:T(8,128)(2,1)S(1)}, u32[]{:S(2)}, u32[]{:S(2)}) collective-permute-start(bf16[48,1280]{1,0:T(8,128)(2,1)S(1)} %fusion.25), channel_id=1, source_target_pairs={{12,11},{13,8},{14,9},{15,10},{28,27},{29,24},{30,25},{31,26},{44,... | collective-permute-start | bytes 368648 | tf_op jit(solution)/shard_map/ppermute | solution.py:36
  239.4 4.2 %collective-permute-start.20 = (bf16[48,1280]{1,0:T(8,128)(2,1)S(1)}, bf16[48,1280]{1,0:T(8,128)(2,1)S(1)}, u32[]{:S(2)}, u32[]{:S(2)}) collective-permute-start(bf16[48,1280]{1,0:T(8,128)(2,1)S(1)} %fusion.25), channel_id=1, source_target_pairs={{12,10},{13,11},{14,8},{15,9},{28,26},{29,27},{30,24},{31,25},{44,... | collective-permute-start | bytes 368648 | tf_op jit(solution)/shard_map/ppermute | solution.py:36
  241.0 3.7 %collective-permute-start.19 = (bf16[48,1280]{1,0:T(8,128)(2,1)S(1)}, bf16[48,1280]{1,0:T(8,128)(2,1)S(1)}, u32[]{:S(2)}, u32[]{:S(2)}) collective-permute-start(bf16[48,1280]{1,0:T(8,128)(2,1)S(1)} %fusion.25), channel_id=1, source_target_pairs={{12,9},{13,10},{14,11},{15,8},{28,25},{29,26},{30,27},{31,24},{44,... | collective-permute-start | bytes 368648 | tf_op jit(solution)/shard_map/ppermute | solution.py:36
  242.3 3.7 %collective-permute-start.18 = (bf16[48,1280]{1,0:T(8,128)(2,1)S(1)}, bf16[48,1280]{1,0:T(8,128)(2,1)S(1)}, u32[]{:S(2)}, u32[]{:S(2)}) collective-permute-start(bf16[48,1280]{1,0:T(8,128)(2,1)S(1)} %fusion.25), channel_id=1, source_target_pairs={{12,8},{13,9},{14,10},{15,11},{28,24},{29,25},{30,26},{31,27},{44,... | collective-permute-start | bytes 368648 | tf_op jit(solution)/shard_map/ppermute | solution.py:36
  264.4 2.9 collective-permute-start.25
  265.1 2.3 collective-permute-start.24
  265.8 1.6 collective-permute-start.23
  281.6 2.7 collective-permute-start.29
  282.3 2.0 collective-permute-start.28
  294.7 26.4 %all-to-all-start.10 = ((bf16[16,48,512]{2,1,0:T(8,128)(2,1)}), bf16[16,48,512]{2,1,0:T(8,128)(2,1)S(1)}, u32[]{:S(2)}, u32[]{:S(2)}) async-start(bf16[16,48,512]{2,1,0:T(8,128)(2,1)} %fusion.9), calls=%async_computation.11 | async-start | bytes 1572864 | tf_op jit(solution)/shard_map/all_to_all | solution.py:446
  (25 other events, 265.0 us)
Sparse Core Ops, SparseCore 0:
  10.4 44.4 all-gather.1
  204.0 71.6 reduce-scatter.2
  290.2 69.8 reduce-scatter.4
